TPU v7x, 32 devices: a whole 2x2x4 slice. The times are simulated.
32 devices in a mesh: dp: 4 (over x, core), fsdp: 8 (over z, y).
Axes of the slice: x: 2, y: 2, z: 4, core: 2. Of those that a mesh axis runs over, the one named last changes fastest.
Arguments:
- tokens: bfloat16 [1024, 4096], P(('dp', 'fsdp')), may hold values from -6 to 6
- cotangent: bfloat16 [1024, 4096], P(('dp', 'fsdp')), may hold values from -2 to 2
- gate_base: bfloat16 [4096, 10240], P(None, 'fsdp'), may hold values from -0.09375 to 0.09375
- up_base: bfloat16 [4096, 10240], P(None, 'fsdp'), may hold values from -0.09375 to 0.09375
- out_base: bfloat16 [10240, 4096], P('fsdp'), may hold values from -0.0625 to 0.0625
- subspace: float32 [512, 128], P('fsdp'), may hold values from -6 to 6
- sign_flips: int32 [2, 512, 128, 640], P(None, 'fsdp'), may hold values from -1 to 1, as said below
- fast_gains: bfloat16 [2, 512, 128, 640], P(None, None, 'fsdp'), may hold values from -5 to 5
- fast_scales: float32 [2, 512, 640], P(None, 'fsdp'), may hold values from 0.5 to 2
- block_orders: int32 [2, 512], replicated, may hold values from 0 to 511, each once within a row
Outputs:
- subspace_grad: float32 [512, 128], P('fsdp')
Inputs may be any that keep to these rules, and one draw needn't show every extreme that they name: `sign_flips`: each entry is -1 or +1.
All inputs are finite; a program needn't handle non-finite values.
Results may differ from a plain program's by a relative error of at most 0.017.
Values may be sent and summed in bfloat16 or wider, within the bound.
A program may use at most 384 MiB of HBM per device.

v0:
```python
import jax
import jax.numpy as jnp
from jax import lax
from jax.sharding import PartitionSpec as P

D = 4096
FF = 10240


def hadamard(size, dtype):
    index = jnp.arange(size, dtype=jnp.int32)
    anded = jnp.bitwise_and(index[:, None], index[None, :])
    parity = jnp.zeros((size, size), jnp.int32)
    for bit in range(max(size.bit_length() - 1, 0)):
        parity = jnp.bitwise_xor(parity, jnp.bitwise_and(jnp.right_shift(anded, bit), 1))
    return (1 - 2 * parity).astype(dtype)


def gelu_tanh(value):
    argument = 0.7978845608028654 * (value + 0.044715 * value * value * value)
    return 0.5 * value * (1.0 + jnp.tanh(argument))


def gelu_slope(value):
    argument = 0.7978845608028654 * (value + 0.044715 * value * value * value)
    tangent = jnp.tanh(argument)
    return 0.5 * (1.0 + tangent) + 0.5 * value * (1.0 - tangent * tangent) * 0.7978845608028654 * (
        1.0 + 0.134145 * value * value
    )


def contract(left, right, left_dim, right_dim):
    return lax.dot_general(
        left, right, (((left_dim,), (right_dim,)), ((), ())), preferred_element_type=jnp.float32
    )


def local_spread(signs, subspace):
    inner, width = (signs.shape[0], signs.shape[1])
    highest = lax.Precision.HIGHEST
    lifted = signs.astype(jnp.float32) * subspace[:, :, None]
    lifted = jnp.einsum("dc,ack->adk", hadamard(width, jnp.float32), lifted, precision=highest)
    lifted = jnp.einsum("ba,ack->bck", hadamard(inner, jnp.float32), lifted, precision=highest)
    return (lifted * (inner * width) ** (-0.5)).astype(jnp.bfloat16)


def middle_forward(first, gains, order, parts):
    blocks_all, columns, vectors = first.shape
    grouped = first.reshape(parts, blocks_all // parts, columns, vectors)
    turned = jnp.einsum(
        "qp,pack->qack", hadamard(parts, jnp.bfloat16), grouped, preferred_element_type=jnp.float32
    )
    turned = (turned * parts ** (-0.5)).reshape(blocks_all, columns, vectors)
    mixed = (gains.astype(jnp.float32) * jnp.take(turned, order, axis=0)).astype(jnp.bfloat16)
    second = jnp.einsum(
        "cb,bxk->cxk", hadamard(blocks_all, jnp.bfloat16), mixed, preferred_element_type=jnp.float32
    )
    return (second * blocks_all ** (-0.5)).astype(jnp.bfloat16)


def local_finish(second, scales, factor):
    width = second.shape[1]
    wide = jnp.einsum(
        "dc,ack->adk", hadamard(width, jnp.bfloat16), second, preferred_element_type=jnp.float32
    )
    return wide * (scales[:, None, :] * (factor * width ** (-0.5)))


def local_gather_back(grads, scales, factor):
    width = grads.shape[1]
    scaled = grads * (scales[:, None, :] * (factor * width ** (-0.5)))
    back = jnp.einsum(
        "dc,ack->adk", hadamard(width, jnp.float32), scaled, precision=lax.Precision.HIGHEST
    )
    return back.astype(jnp.bfloat16)


def middle_adjoint(back, gains, order, parts):
    blocks_all, columns, vectors = back.shape
    spread = jnp.einsum(
        "cb,bxk->cxk", hadamard(blocks_all, jnp.bfloat16), back, preferred_element_type=jnp.float32
    )
    spread = (gains.astype(jnp.float32) * (spread * blocks_all ** (-0.5))).astype(jnp.bfloat16)
    inverse = (
        jnp.zeros((blocks_all,), jnp.int32).at[order].set(jnp.arange(blocks_all, dtype=jnp.int32))
    )
    reverted = jnp.take(spread, inverse, axis=0).reshape(
        parts, blocks_all // parts, columns, vectors
    )
    folded = jnp.einsum(
        "qp,pack->qack", hadamard(parts, jnp.bfloat16), reverted, preferred_element_type=jnp.float32
    )
    return (folded * parts ** (-0.5)).reshape(blocks_all, columns, vectors).astype(jnp.bfloat16)


def local_adjoint_finish(folded, signs):
    inner, width = (signs.shape[0], signs.shape[1])
    wide = jnp.einsum(
        "dc,ack->adk", hadamard(width, jnp.bfloat16), folded, preferred_element_type=jnp.float32
    )
    wide = jnp.einsum(
        "ba,ack->bck", hadamard(inner, jnp.float32), wide, precision=lax.Precision.HIGHEST
    )
    wide = wide * (inner * width) ** (-0.5)
    return jnp.sum(signs.astype(jnp.float32) * wide, axis=2)


def on_device(
    tokens,
    cotangent,
    gate_base,
    up_base,
    out_base,
    subspace,
    sign_flips,
    fast_gains,
    fast_scales,
    block_orders,
):
    parts = lax.axis_size("fsdp")
    whole_x, whole_dy = (
        lax.all_gather(tokens, "fsdp", axis=0, tiled=True),
        lax.all_gather(cotangent, "fsdp", axis=0, tiled=True),
    )
    factors = (D ** (-0.5), FF ** (-0.5))
    layout = sign_flips.shape[1:]
    base_gate = gate_base.reshape(layout)
    base_out = out_base.reshape(layout)
    signs_fwd, gains_fwd, scales_fwd = (sign_flips, fast_gains, fast_scales)
    firsts = [local_spread(signs_fwd[which], subspace) for which in range(2)]
    turned = [
        lax.all_to_all(item, "fsdp", split_axis=1, concat_axis=0, tiled=True) for item in firsts
    ]
    seconds = [
        middle_forward(turned[which], gains_fwd[which], block_orders[which], parts)
        for which in range(2)
    ]
    returned = [
        lax.all_to_all(item, "fsdp", split_axis=0, concat_axis=1, tiled=True) for item in seconds
    ]
    deltas = [
        local_finish(returned[which], scales_fwd[which], factors[which]) for which in range(2)
    ]
    gate_weight = (base_gate + deltas[0]).astype(jnp.bfloat16)
    out_weight = (base_out + deltas[1]).astype(jnp.bfloat16)
    gate_weight = gate_weight.reshape(gate_base.shape)
    out_weight = out_weight.reshape(out_base.shape)
    gate = jnp.dot(whole_x, gate_weight, preferred_element_type=jnp.float32)
    up = jnp.dot(whole_x, up_base, preferred_element_type=jnp.float32)
    hidden = (gelu_tanh(gate) * up).astype(jnp.bfloat16)
    hidden_grad = contract(whole_dy, out_weight, 1, 1)
    gate_grad = (hidden_grad * up * gelu_slope(gate)).astype(jnp.bfloat16)
    out_grad = contract(hidden, whole_dy, 0, 0)
    in_grad = contract(whole_x, gate_grad, 0, 0)
    grads = (in_grad.reshape(layout), out_grad.reshape(layout))
    shared = lax.psum((grads[0], grads[1]), "dp")
    signs_used, gains_used, scales_used = (sign_flips, fast_gains, fast_scales)
    backs = [
        local_gather_back(shared[which], scales_used[which], factors[which]) for which in range(2)
    ]
    moved = [
        lax.all_to_all(item, "fsdp", split_axis=1, concat_axis=0, tiled=True) for item in backs
    ]
    foldeds = [
        middle_adjoint(moved[which], gains_used[which], block_orders[which], parts)
        for which in range(2)
    ]
    homed = [
        lax.all_to_all(item, "fsdp", split_axis=0, concat_axis=1, tiled=True) for item in foldeds
    ]
    result = local_adjoint_finish(homed[0], signs_used[0]) + local_adjoint_finish(
        homed[1], signs_used[1]
    )
    return result


def solution(mesh):
    in_specs = (
        P(("dp", "fsdp"), None),
        P(("dp", "fsdp"), None),
        P(None, "fsdp"),
        P(None, "fsdp"),
        P("fsdp", None),
        P("fsdp", None),
        P(None, "fsdp", None, None),
        P(None, None, "fsdp", None),
        P(None, "fsdp", None),
        P(),
    )
    out_specs = P("fsdp", None)
    return jax.shard_map(
        on_device, mesh=mesh, in_specs=in_specs, out_specs=out_specs, check_vma=False
    )
```

profile of v0, /device:TPU:0, one launch (start us, length us, event | category | flops | bytes accessed | tf_op | source)
XLA Modules:
  0.0 3065.6 jit_solution(15479640530343102700)
XLA Ops:
  6.5 29.3 fusion.270
  35.9 28.9 fusion.16
  64.8 43.8 %fusion.45 = f32[64,128,640]{1,2,0:T(8,128)} fusion(f32[64,128,640]{2,0,1:T(8,128)S(1)} %get-tuple-element.15), kind=kOutput, calls=%fused_computation.70 | convolution fusion | flops 8053456896 | bytes 41943040 | tf_op jit(solution)/shard_map/dc,ack->adk/dot_general | solution.py:42
  108.6 21.9 copy.125
  130.6 25.2 multiply_convert_fusion.3
  163.5 48.6 %fusion.42 = f32[64,128,640]{1,2,0:T(8,128)} fusion(f32[64,128,640]{2,0,1:T(8,128)} %get-tuple-element.16), kind=kOutput, calls=%fused_computation.69 | convolution fusion | flops 8053456896 | bytes 41943040 | tf_op jit(solution)/shard_map/dc,ack->adk/dot_general | solution.py:42
  212.1 21.9 copy.114
  234.0 25.1 multiply_convert_fusion.5
  259.1 132.5 %all-to-all-done.2 = bf16[64,128,640]{2,0,1:T(8,128)(2,1)} async-done(((bf16[64,128,640]{2,0,1:T(8,128)(2,1)}), bf16[64,128,640]{2,0,1:T(8,128)(2,1)}, u32[]{:S(2)}, u32[]{:S(2)}) %all-to-all-start.2) | async-done | bytes 10485792 | tf_op jit(solution)/shard_map/all_to_all | solution.py:132
  396.7 17.3 fusion.271
  414.1 24.2 broadcast_multiply_fusion
  438.3 19.4 copy.127
  457.6 18.2 gather_fusion.1
  475.9 23.4 multiply_convert_fusion.2
  499.2 13.9 copy.129
  513.1 110.7 %all-to-all-done = bf16[64,128,640]{2,0,1:T(8,128)(2,1)} async-done(((bf16[64,128,640]{2,0,1:T(8,128)(2,1)}), bf16[64,128,640]{2,0,1:T(8,128)(2,1)}, u32[]{:S(2)}, u32[]{:S(2)}) %all-to-all-start) | async-done | bytes 10485792 | tf_op jit(solution)/shard_map/all_to_all | solution.py:132
  629.2 24.2 broadcast_multiply_fusion.1
  653.4 19.4 copy.116
  672.8 18.2 gather_fusion
  691.0 23.7 multiply_convert_fusion.4
  714.7 14.0 copy.118
  728.7 127.0 %all-to-all-done.3 = bf16[512,16,640]{2,1,0:T(8,128)(2,1)} async-done(((bf16[512,16,640]{2,1,0:T(8,128)(2,1)}), bf16[512,16,640]{2,1,0:T(8,128)(2,1)}, u32[]{:S(2)}, u32[]{:S(2)}) %all-to-all-start.3) | async-done | bytes 10485792 | tf_op jit(solution)/shard_map/all_to_all | solution.py:139
  862.4 17.5 reshape.140
  879.9 22.6 copy.132
  902.5 19.8 reshape.138
  922.3 22.6 copy.121
  944.9 122.8 %all-gather.5.cloned.1.call-done = bf16[256,4096]{1,0:T(8,128)(2,1)} async-done(((bf16[32,4096]{1,0:T(8,128)(2,1)}), bf16[256,4096]{1,0:T(8,128)(2,1)}) %all-gather.5.cloned.1.call-update) | async-done | bytes 2097168 | tf_op jit(solution)/shard_map/all_gather | solution.py:122
  1075.2 9.8 copy.130
  1084.9 16.5 fusion.6
  1101.4 14.5 copy.133
  1115.9 16.0 reshape.132
  1131.9 9.7 copy.119
  1141.6 16.5 fusion.7
  1158.1 14.5 copy.122
  1172.6 18.4 reshape.130
  1197.8 19.6 convolution_bitcast_fusion
  1217.4 22.5 copy.134
  1239.9 22.9 reshape.133
  1262.8 10.1 fusion.68
  1272.9 21.6 reshape.135
  1294.5 22.5 copy.146
  1317.1 692.6 %all-reduce.3.cloned.1.call-done = (f32[64,128,640]{2,1,0:T(8,128)}, f32[64,128,640]{1,2,0:T(8,128)}) async-done(((f32[64,128,640]{2,1,0:T(8,128)}, f32[64,128,640]{1,2,0:T(8,128)}), (f32[64,128,640]{2,1,0:T(8,128)}, f32[64,128,640]{1,2,0:T(8,128)})) %all-reduce.3.cloned.1.call-update) | async-done | bytes 41943056 | tf_op jit(solution)/shard_map/psum | solution.py:156
  2009.7 21.2 convert_bitcast_fusion
  2030.9 15.7 copy.147
  2052.2 37.1 %convert_bitcast_fusion.1 = bf16[64,128,640]{1,2,0:T(8,128)(2,1)} fusion(f32[64,128,640]{2,1,0:T(8,128)} %get-tuple-element.6, f32[64,640]{1,0:T(8,128)S(1)} %copy-done.3), kind=kOutput, calls=%fused_computation.61 | convolution fusion | flops 8063942656 | bytes 31621120 | tf_op jit(solution)/shard_map/dc,ack->adk/dot_general | solution.py:72
  2089.4 15.5 copy.136
  2104.8 175.8 %all-to-all-done.6 = bf16[64,128,640]{2,0,1:T(8,128)(2,1)} async-done(((bf16[64,128,640]{2,0,1:T(8,128)(2,1)}), bf16[64,128,640]{2,0,1:T(8,128)(2,1)}, u32[]{:S(2)}, u32[]{:S(2)}) %all-to-all-start.6) | async-done | bytes 10485792 | tf_op jit(solution)/shard_map/all_to_all | solution.py:162
  2298.1 17.8 fusion.3
  2315.9 14.0 copy.150
  2329.9 18.8 gather_fusion.3
  2372.6 141.1 %all-to-all-done.4 = bf16[64,128,640]{2,0,1:T(8,128)(2,1)} async-done(((bf16[64,128,640]{2,0,1:T(8,128)(2,1)}), bf16[64,128,640]{2,0,1:T(8,128)(2,1)}, u32[]{:S(2)}, u32[]{:S(2)}) %all-to-all-start.4) | async-done | bytes 10485792 | tf_op jit(solution)/shard_map/all_to_all | solution.py:162
  2530.7 18.0 fusion.1
  2548.7 14.0 copy.139
  2562.6 19.0 gather_fusion.2
  2605.4 140.2 %all-to-all-done.7 = bf16[512,16,640]{2,1,0:T(8,128)(2,1)} async-done(((bf16[512,16,640]{2,1,0:T(8,128)(2,1)}), bf16[512,16,640]{2,1,0:T(8,128)(2,1)}, u32[]{:S(2)}, u32[]{:S(2)}) %all-to-all-start.7) | async-done | bytes 10485792 | tf_op jit(solution)/shard_map/all_to_all | solution.py:169
  2750.9 9.6 copy.153
  2760.6 11.0 convolution_bitcast_fusion.1
  2771.6 21.9 copy.155
  2793.5 37.7 %multiply_reduce_fusion = f32[64,128]{0,1:T(8,128)S(1)} fusion(s32[1,64,128,640]{3,2,1,0:T(8,128)} %get-tuple-element.9, f32[64,128,640]{2,0,1:T(8,128)} %copy.155), kind=kOutput, calls=%fused_computation.28 | convolution fusion | flops 4047581184 | bytes 41975808 | tf_op jit(solution)/shard_map/ba,ack->bck/dot_general | solution.py:101
  2831.2 146.8 %all-to-all-done.5 = bf16[512,16,640]{2,1,0:T(8,128)(2,1)} async-done(((bf16[512,16,640]{2,1,0:T(8,128)(2,1)}), bf16[512,16,640]{2,1,0:T(8,128)(2,1)}, u32[]{:S(2)}, u32[]{:S(2)}) %all-to-all-start.5) | async-done | bytes 10485792 | tf_op jit(solution)/shard_map/all_to_all | solution.py:169
  2978.0 9.7 copy.142
  2987.7 11.1 convolution_bitcast_fusion.2
  2998.7 21.9 copy.144
  3020.6 37.5 %multiply_reduce_fusion.1 = f32[64,128]{0,1:T(8,128)S(1)} fusion(s32[1,64,128,640]{3,2,1,0:T(8,128)} %get-tuple-element.10, f32[64,128,640]{2,0,1:T(8,128)} %copy.144), kind=kOutput, calls=%fused_computation.32 | convolution fusion | flops 4047581184 | bytes 41975808 | tf_op jit(solution)/shard_map/ba,ack->bck/dot_general | solution.py:101
  (68 shorter events, 133.0 us)
Async XLA Ops:
  6.5 29.3 copy-start.7
  155.8 235.8 %all-to-all-start.2 = ((bf16[64,128,640]{2,0,1:T(8,128)(2,1)}), bf16[64,128,640]{2,0,1:T(8,128)(2,1)}, u32[]{:S(2)}, u32[]{:S(2)}) async-start(bf16[64,128,640]{2,0,1:T(8,128)(2,1)} %multiply_convert_fusion.3), calls=%async_computation.2 | async-start | bytes 20971520 | tf_op jit(solution)/shard_map/all_to_all | solution.py:132
  259.1 137.6 %copy-start.8 = (s32[2,512]{1,0:T(2,128)S(1)}, s32[2,512]{1,0:T(2,128)}, u32[]{:S(2)}) copy-start(s32[2,512]{1,0:T(2,128)} %param.23) | copy-start | bytes 12292
  391.5 232.3 %all-to-all-start = ((bf16[64,128,640]{2,0,1:T(8,128)(2,1)}), bf16[64,128,640]{2,0,1:T(8,128)(2,1)}, u32[]{:S(2)}, u32[]{:S(2)}) async-start(bf16[64,128,640]{2,0,1:T(8,128)(2,1)} %multiply_convert_fusion.5), calls=%async_computation | async-start | bytes 20971520 | tf_op jit(solution)/shard_map/all_to_all | solution.py:132
  623.8 231.9 %all-to-all-start.3 = ((bf16[512,16,640]{2,1,0:T(8,128)(2,1)}), bf16[512,16,640]{2,1,0:T(8,128)(2,1)}, u32[]{:S(2)}, u32[]{:S(2)}) async-start(bf16[512,16,640]{2,1,0:T(8,128)(2,1)} %copy.129), calls=%async_computation.3 | async-start | bytes 20971520 | tf_op jit(solution)/shard_map/all_to_all | solution.py:139
  855.7 276.2 %all-to-all-start.1 = ((bf16[512,16,640]{2,1,0:T(8,128)(2,1)}), bf16[512,16,640]{2,1,0:T(8,128)(2,1)}, u32[]{:S(2)}, u32[]{:S(2)}) async-start(bf16[512,16,640]{2,1,0:T(8,128)(2,1)} %copy.118), calls=%async_computation.1 | async-start | bytes 20971520 | tf_op jit(solution)/shard_map/all_to_all | solution.py:139
  860.8 206.8 %all-gather.5.cloned.1.call-start = ((), (), s32[]{:S(2)}) async-start(), calls=%async_computation.9 | async-start | bytes 2359296 | tf_op jit(solution)/shard_map/all_gather | solution.py:122
  861.6 336.2 %all-gather.3.cloned.1.call-start = ((), (), s32[]{:S(2)}) async-start(), calls=%async_computation.8 | async-start | bytes 2359296 | tf_op jit(solution)/shard_map/all_gather | solution.py:123
  862.3 1147.4 %all-reduce.3.cloned.1.call-start = ((), (), s32[]{:S(2)}) async-start(), calls=%async_computation.10 | async-start | bytes 83886080 | tf_op jit(solution)/shard_map/psum | solution.py:156
  922.3 22.6 copy-start.6
  944.9 140.0 %copy-start.2 = (f32[64,640]{1,0:T(8,128)}, f32[64,640]{1,0:T(8,128)S(1)}, u32[]{:S(2)}) copy-start(f32[64,640]{1,0:T(8,128)S(1)} %get-tuple-element.13) | copy-start | bytes 491524
  944.9 196.7 %copy-start.4 = (f32[64,640]{1,0:T(8,128)}, f32[64,640]{1,0:T(8,128)S(1)}, u32[]{:S(2)}) copy-start(f32[64,640]{1,0:T(8,128)S(1)} %get-tuple-element.14) | copy-start | bytes 491524
  1197.8 19.6 copy-start.1
  1239.9 22.9 copy-start
  1317.0 692.7 %copy-start.5 = (f32[64,640]{1,0:T(8,128)S(1)}, f32[64,640]{1,0:T(8,128)}, u32[]{:S(2)}) copy-start(f32[64,640]{1,0:T(8,128)} %copy-done.4) | copy-start | bytes 491524
  2046.6 5.7 copy-start.3
  2046.6 234.1 %all-to-all-start.6 = ((bf16[64,128,640]{2,0,1:T(8,128)(2,1)}), bf16[64,128,640]{2,0,1:T(8,128)(2,1)}, u32[]{:S(2)}, u32[]{:S(2)}) async-start(bf16[64,128,640]{2,0,1:T(8,128)(2,1)} %copy.147), calls=%async_computation.6 | async-start | bytes 20971520 | tf_op jit(solution)/shard_map/all_to_all | solution.py:162
  2104.8 181.4 %copy-start.9 = (s32[2,512]{1,0:T(2,128)S(1)}, s32[2,512]{1,0:T(2,128)}, u32[]{:S(2)}) copy-start(s32[2,512]{1,0:T(2,128)} %param.23) | copy-start | bytes 12292
  2280.7 233.0 %all-to-all-start.4 = ((bf16[64,128,640]{2,0,1:T(8,128)(2,1)}), bf16[64,128,640]{2,0,1:T(8,128)(2,1)}, u32[]{:S(2)}, u32[]{:S(2)}) async-start(bf16[64,128,640]{2,0,1:T(8,128)(2,1)} %copy.136), calls=%async_computation.4 | async-start | bytes 20971520 | tf_op jit(solution)/shard_map/all_to_all | solution.py:162
  2513.7 231.9 %all-to-all-start.7 = ((bf16[512,16,640]{2,1,0:T(8,128)(2,1)}), bf16[512,16,640]{2,1,0:T(8,128)(2,1)}, u32[]{:S(2)}, u32[]{:S(2)}) async-start(bf16[512,16,640]{2,1,0:T(8,128)(2,1)} %bitcast.196), calls=%async_computation.7 | async-start | bytes 20971520 | tf_op jit(solution)/shard_map/all_to_all | solution.py:169
  2745.6 232.4 %all-to-all-start.5 = ((bf16[512,16,640]{2,1,0:T(8,128)(2,1)}), bf16[512,16,640]{2,1,0:T(8,128)(2,1)}, u32[]{:S(2)}, u32[]{:S(2)}) async-start(bf16[512,16,640]{2,1,0:T(8,128)(2,1)} %bitcast.197), calls=%async_computation.5 | async-start | bytes 20971520 | tf_op jit(solution)/shard_map/all_to_all | solution.py:169
Sparse Core Ops, SparseCore 0:
  863.8 203.8 all-gather.4
  1069.8 77.6 all-gather.2
  1317.2 692.4 all-reduce.2
where the time goes:
time: 3080 us; the launch traced here: 3070 us
  waiting for transfers between devices  1790 us (58%)
  local copies, waits for them, and re-layouts  651 us (21%)
  matrix products  523 us (17%)
  starting transfers between devices  45.2 us (1%)
  other arithmetic  41.5 us (1%)
    psum x1, waiting for transfers between devices, on_device(): shared = lax.psum((grads[0], grads[1]), 'dp')  693 us
    all_to_all x4, waiting for transfers between devices, on_device(): lax.all_to_all(item, 'fsdp', split_axis=1, concat_axis=0, tiled=True)  560 us
    all_to_all x4, waiting for transfers between devices, on_device(): lax.all_to_all(item, 'fsdp', split_axis=0, concat_axis=1, tiled=True)  414 us
    all_gather x1, waiting for transfers between devices, on_device(): lax.all_gather(tokens, 'fsdp', axis=0, tiled=True)  123 us
    dot_general x2, matrix products, local_spread(): jnp.einsum('dc,ack->adk', hadamard(width, jnp.float32), lifted, precision...  92.4 us
    dot_general x2, matrix products, local_adjoint_finish(): jnp.einsum('ba,ack->bck', hadamard(inner, jnp.float32), wide, precision=l...  75.2 us
    reshape x3, local copies, waits for them, and re-layouts, on_device(): grads = (in_grad.reshape(layout), out_grad.reshape(layout))  67.1 us
  transfers between devices with their start and end apart: 11, of which 9 were waited for; matrix products, arithmetic and copies ran while one was open for 27% of the time, Pallas kernels for 0%

commit v1 on v0

v1 whole, which is shorter than its diff:
```python
import jax
import jax.numpy as jnp
from jax import lax
from jax.sharding import PartitionSpec as P

D = 4096
FF = 10240


def hadamard(size, dtype):
    index = jnp.arange(size, dtype=jnp.int32)
    anded = jnp.bitwise_and(index[:, None], index[None, :])
    parity = jnp.zeros((size, size), jnp.int32)
    for bit in range(max(size.bit_length() - 1, 0)):
        parity = jnp.bitwise_xor(parity, jnp.bitwise_and(jnp.right_shift(anded, bit), 1))
    return (1 - 2 * parity).astype(dtype)


def gelu_pair(value):
    argument = 0.7978845608028654 * (value + 0.044715 * value * value * value)
    tangent = jnp.tanh(argument)
    slope = 0.5 * (1.0 + tangent) + 0.5 * value * (1.0 - tangent * tangent) * 0.7978845608028654 * (
        1.0 + 0.134145 * value * value
    )
    return 0.5 * value * (1.0 + tangent), slope


def contract(left, right, left_dim, right_dim):
    return lax.dot_general(
        left, right, (((left_dim,), (right_dim,)), ((), ())), preferred_element_type=jnp.float32
    )


def turning(order, blocks_all, parts):
    inner = blocks_all // parts
    column = jnp.arange(blocks_all, dtype=jnp.int32)[None, :]
    row = order[:, None]
    anded = jnp.bitwise_and(row // inner, column // inner)
    parity = jnp.zeros(anded.shape, jnp.int32)
    for bit in range(max(parts.bit_length() - 1, 0)):
        parity = jnp.bitwise_xor(parity, jnp.bitwise_and(jnp.right_shift(anded, bit), 1))
    return jnp.where(row % inner == column % inner, 1 - 2 * parity, 0).astype(jnp.bfloat16)


def local_spread(signs, subspace):
    inner, width, _ = signs.shape
    lifted = signs * subspace.astype(jnp.bfloat16)[:, :, None]
    lifted = jnp.einsum(
        "dc,ack->adk", hadamard(width, jnp.bfloat16), lifted, preferred_element_type=jnp.float32
    ).astype(jnp.bfloat16)
    lifted = jnp.einsum(
        "ba,ack->bck", hadamard(inner, jnp.bfloat16), lifted, preferred_element_type=jnp.float32
    )
    return (lifted * (inner * width) ** (-0.5)).astype(jnp.bfloat16)


def to_columns(item, parts):
    inner, width, vectors = item.shape
    cut = item.reshape(inner, parts, (width // parts) * vectors).transpose(1, 0, 2)
    moved = lax.all_to_all(cut, "fsdp", split_axis=0, concat_axis=0, tiled=True)
    return moved.reshape(parts * inner, (width // parts) * vectors)


def to_blocks(item, parts, vectors):
    blocks_all, wide = item.shape
    inner, some = blocks_all // parts, wide // vectors
    moved = lax.all_to_all(
        item.reshape(parts, inner, wide), "fsdp", split_axis=0, concat_axis=0, tiled=True
    )
    moved = moved.reshape(parts, inner, some, vectors).transpose(1, 0, 2, 3)
    return moved.reshape(inner, parts * some, vectors)


def middle_forward(first, gains, turn, parts):
    blocks_all = first.shape[0]
    turned = contract(turn, first, 1, 0) * parts ** (-0.5)
    mixed = (gains.astype(jnp.float32) * turned).astype(jnp.bfloat16)
    second = contract(hadamard(blocks_all, jnp.bfloat16), mixed, 1, 0)
    return (second * blocks_all ** (-0.5)).astype(jnp.bfloat16)


def middle_adjoint(back, gains, turn, parts):
    blocks_all = back.shape[0]
    spread = contract(hadamard(blocks_all, jnp.bfloat16), back, 1, 0) * blocks_all ** (-0.5)
    spread = (gains.astype(jnp.float32) * spread).astype(jnp.bfloat16)
    folded = contract(turn, spread, 0, 0)
    return (folded * parts ** (-0.5)).astype(jnp.bfloat16)


def local_finish(second, scales, factor):
    width = second.shape[1]
    wide = jnp.einsum(
        "dc,ack->adk", hadamard(width, jnp.bfloat16), second, preferred_element_type=jnp.float32
    )
    return wide * (scales[:, None, :] * (factor * width ** (-0.5)))


def local_gather_back(grads, scales, factor):
    width = grads.shape[1]
    scaled = (grads * (scales[:, None, :] * (factor * width ** (-0.5)))).astype(jnp.bfloat16)
    back = jnp.einsum(
        "dc,ack->adk", hadamard(width, jnp.bfloat16), scaled, preferred_element_type=jnp.float32
    )
    return back.astype(jnp.bfloat16)


def local_adjoint_finish(folded, signs):
    inner, width, _ = signs.shape
    wide = jnp.einsum(
        "dc,ack->adk", hadamard(width, jnp.bfloat16), folded, preferred_element_type=jnp.float32
    ).astype(jnp.bfloat16)
    wide = jnp.einsum(
        "ba,ack->bck", hadamard(inner, jnp.bfloat16), wide, preferred_element_type=jnp.float32
    )
    return jnp.sum(signs.astype(jnp.float32) * wide, axis=2) * (inner * width) ** (-0.5)


def on_device(
    tokens,
    cotangent,
    gate_base,
    up_base,
    out_base,
    subspace,
    sign_flips,
    fast_gains,
    fast_scales,
    block_orders,
):
    parts, groups = lax.axis_size("fsdp"), lax.axis_size("dp")
    mine = lax.axis_index("dp")
    _, inner, width, vectors = sign_flips.shape
    blocks_all, some = fast_gains.shape[1], fast_gains.shape[2]
    share = vectors // groups
    hidden_here = gate_base.shape[1]
    direct = hidden_here % vectors == 0
    runs = hidden_here // vectors if direct else 1
    piece = hidden_here // (runs * groups)
    owned = runs * piece

    x, dy = tokens, cotangent
    for axis in ("fsdp", "dp"):
        x = lax.all_gather(x, axis, axis=0, tiled=True)
        dy = lax.all_gather(dy, axis, axis=0, tiled=True)

    factors = (D ** (-0.5), FF ** (-0.5))
    slab = (inner, width, vectors)

    def k_slice(item):
        return lax.dynamic_slice_in_dim(item, mine * share, share, axis=item.ndim - 1)

    def hidden_columns(item):
        cut = item.reshape(item.shape[0], runs, groups, piece)
        cut = lax.dynamic_index_in_dim(cut, mine, 2, keepdims=False)
        return cut.reshape(item.shape[0], owned)

    signs = k_slice(sign_flips).astype(jnp.bfloat16)
    gains = k_slice(fast_gains).reshape(2, blocks_all, some * share)
    scales = k_slice(fast_scales)
    turns = [turning(block_orders[which], blocks_all, parts) for which in range(2)]

    def expand(which):
        first = local_spread(signs[which], subspace)
        second = middle_forward(to_columns(first, parts), gains[which], turns[which], parts)
        return local_finish(to_blocks(second, parts, share), scales[which], factors[which])

    delta_gate = expand(0)
    if direct:
        base_gate = hidden_columns(gate_base).reshape(inner, width, share)
        gate_weight = (base_gate + delta_gate).astype(jnp.bfloat16).reshape(D, owned)
    else:
        base_gate = k_slice(gate_base.reshape(slab))
        gate_weight = (base_gate + delta_gate).astype(jnp.bfloat16)
        gate_weight = lax.all_gather(gate_weight, "dp", axis=2, tiled=True)
        gate_weight = hidden_columns(gate_weight.reshape(gate_base.shape))

    strip = inner // (runs * groups)
    delta_out = expand(1).astype(jnp.bfloat16).reshape(runs, groups, strip, width, share)
    delta_out = lax.all_to_all(delta_out, "dp", split_axis=1, concat_axis=4, tiled=True)
    base_out = lax.dynamic_index_in_dim(
        out_base.reshape(runs, groups, piece, D), mine, 1, keepdims=False
    )
    out_weight = base_out.reshape(owned, D) + delta_out.reshape(owned, D)

    gate = jnp.dot(x, gate_weight, preferred_element_type=jnp.float32)
    up = jnp.dot(x, hidden_columns(up_base), preferred_element_type=jnp.float32)
    bent, slope = gelu_pair(gate)
    hidden = (bent * up).astype(jnp.bfloat16)
    hidden_grad = contract(dy, out_weight, 1, 1)
    gate_grad = (hidden_grad * up * slope).astype(jnp.bfloat16)

    out_grad = contract(hidden, dy, 0, 0).reshape(runs, strip, width, vectors)
    strips = lax.dynamic_index_in_dim(
        fast_scales[1].reshape(runs, groups, strip, vectors), mine, 1, keepdims=False
    )
    back_out = local_gather_back(
        out_grad.reshape(runs * strip, width, vectors),
        strips.reshape(runs * strip, vectors),
        factors[1],
    )
    back_out = lax.all_to_all(
        back_out.reshape(runs, 1, strip, width, vectors), "dp", split_axis=4, concat_axis=1, tiled=True
    ).reshape(inner, width, share)

    in_grad = contract(x, gate_grad, 0, 0)
    if direct:
        in_grad = in_grad.reshape(inner, width, share)
    else:
        in_grad = lax.all_gather(in_grad.astype(jnp.bfloat16), "dp", axis=1, tiled=True)
        in_grad = k_slice(in_grad.reshape(slab)).astype(jnp.float32)
    back_gate = local_gather_back(in_grad, scales[0], factors[0])

    def fold(back, which):
        folded = middle_adjoint(to_columns(back, parts), gains[which], turns[which], parts)
        return local_adjoint_finish(to_blocks(folded, parts, share), signs[which])

    result = fold(back_out, 1) + fold(back_gate, 0)
    return lax.psum(result, "dp")


def solution(mesh):
    in_specs = (
        P(("dp", "fsdp"), None),
        P(("dp", "fsdp"), None),
        P(None, "fsdp"),
        P(None, "fsdp"),
        P("fsdp", None),
        P("fsdp", None),
        P(None, "fsdp", None, None),
        P(None, None, "fsdp", None),
        P(None, "fsdp", None),
        P(),
    )
    out_specs = P("fsdp", None)
    return jax.shard_map(
        on_device, mesh=mesh, in_specs=in_specs, out_specs=out_specs, check_vma=False
    )
```

time: 3080 us -> 889 us (0.29)
  waiting for transfers between devices: 1790 us -> 355 us
  matrix products: 523 us -> 105 us
  local copies, waits for them, and re-layouts: 651 us -> 327 us
    psum x1 -> x0, waiting for transfers between devices: 693 us -> none  [on_device(): shared = lax.psum((grads[0], grads[1]), 'dp')]
    all_to_all x8 -> x10, waiting for transfers between devices: 974 us -> 299 us  [the longest x4 154 us: to_columns(): moved = lax.all_to_all(cut, 'fsdp', split_axis=0, concat_axis=0, tiled=True)]
    dot_general x20 -> x8, matrix products: 460 us -> 34 us  [the longest x2 9.96 us: local_gather_back(): jnp.einsum('dc,ack->adk', hadamard(width, jnp.bfloat16), scaled, preferre...]
    convert_element_type x12 -> x8, local copies, waits for them, and re-layouts: 186 us -> 62.9 us  [the longest x3 31.6 us: on_device(): base_gate + delta_gate]
    transpose x4, local copies, waits for them, and re-layouts: 87.7 us -> 10.8 us  [to_columns(): item.reshape(inner, parts, width // parts * vectors).transpose(1, 0, 2)]
    gather x4 -> x0, local copies, waits for them, and re-layouts: 74.2 us -> none  [the longest x2 37.8 us: middle_adjoint(): jnp.take(spread, inverse, axis=0)]
    all_gather x2 -> x4, waiting for transfers between devices: 123 us -> 53.5 us  [the longest x2 53.5 us: on_device(): x = lax.all_gather(x, axis, axis=0, tiled=True)]
    unnamed x21, local copies, waits for them, and re-layouts: 0.13 us -> 60.5 us
  transfers between devices with their start and end apart: 11 -> 14, of which waited for: 9 -> 9; matrix products, arithmetic and copies ran while one was open for 27% -> 46% of each run, Pallas kernels for 0% -> 0%
where the time goes in v1:
time: 889 us; the launch traced here: 878 us
  waiting for transfers between devices  355 us (40%)
  local copies, waits for them, and re-layouts  327 us (37%)
  matrix products  105 us (12%)
  starting transfers between devices  41.9 us (5%)
  other arithmetic  24.9 us (3%)
  between operations  13.9 us (2%)
  blocking collectives  10.9 us (1%)
    all_to_all x4, waiting for transfers between devices, to_columns(): moved = lax.all_to_all(cut, 'fsdp', split_axis=0, concat_axis=0, tiled=True)  154 us
    all_to_all x4, waiting for transfers between devices, to_blocks(): lax.all_to_all(item.reshape(parts, inner, wide), 'fsdp', split_axis=0, co...  146 us
    unnamed x21, local copies, waits for them, and re-layouts  60.5 us
    dot_general x6, matrix products, contract(): lax.dot_general(left, right, (((left_dim,), (right_dim,)), ((), ())), pre...  60.1 us
    all_gather x2, waiting for transfers between devices, on_device(): x = lax.all_gather(x, axis, axis=0, tiled=True)  53.5 us
    convert_element_type x3, local copies, waits for them, and re-layouts, on_device(): base_gate + delta_gate  31.6 us
    reshape x4, local copies, waits for them, and re-layouts, to_blocks(): moved = moved.reshape(parts, inner, some, vectors).transpose(1, 0, 2, 3)  31.2 us
    reshape x3, local copies, waits for them, and re-layouts, to_columns(): item.reshape(inner, parts, width // parts * vectors).transpose(1, 0, 2)  24.1 us
  transfers between devices with their start and end apart: 14, of which 9 were waited for; matrix products, arithmetic and copies ran while one was open for 46% of the time, Pallas kernels for 0%

profile of v1, /device:TPU:0, one launch (start us, length us, event | category | flops | bytes accessed | tf_op | source)
XLA Modules:
  0.0 878.0 jit_solution(991944219158051784)
XLA Ops:
  8.1 53.5 %all-gather.5.cloned.1.call-done = bf16[256,4096]{1,0:T(8,128)(2,1)} async-done(((bf16[32,4096]{1,0:T(8,128)(2,1)}), bf16[256,4096]{1,0:T(8,128)(2,1)}) %all-gather.5.cloned.1.call-update) | async-done | bytes 2097168 | tf_op jit(solution)/shard_map/all_gather | solution.py:143
  61.5 14.7 %constant_dynamic-slice_fusion.4 = s32[2,64,128,160]{3,2,1,0:T(8,128)} fusion(s32[2,64,128,640]{3,2,1,0:T(8,128)} %param.16, s32[]{:T(128)S(6)} %select_n.88), kind=kLoop, calls=%fused_computation.170 | loop fusion | bytes 20971524 | tf_op jit(solution)/shard_map/dynamic_slice | solution.py:150
  76.2 15.3 %copy.114 = s32[2,64,128,160]{2,1,3,0:T(8,128)} copy(s32[2,64,128,160]{3,2,1,0:T(8,128)} %constant_dynamic-slice_fusion.4) | data formatting | bytes 20971520
  91.5 7.8 convert_element_type.174
  102.8 6.7 copy.97
  109.4 7.7 reshape.374
  119.4 4.9 all-to-all-start.5
  127.7 6.7 copy.80
  134.4 7.7 reshape.359
  144.4 38.4 %all-to-all-done.5 = bf16[8,64,2560]{2,1,0:T(8,128)(2,1)} async-done(((bf16[8,64,2560]{2,1,0:T(8,128)(2,1)}), bf16[8,64,2560]{2,1,0:T(8,128)(2,1)}, u32[]{:S(2)}, u32[]{:S(2)}) %all-to-all-start.5) | async-done | bytes 2621472 | tf_op jit(solution)/shard_map/all_to_all | solution.py:60
  182.8 4.4 all-to-all-start
  187.3 12.3 %constant_dynamic-slice_fusion.3 = (bf16[1,512,16,160]{3,2,1,0:T(8,128)(2,1)}, bf16[1,512,16,160]{3,2,1,0:T(8,128)(2,1)}) fusion(bf16[2,512,16,640]{3,2,1,0:T(8,128)(2,1)} %param.17, s32[]{:T(128)S(6)} %select_n.88, s32[]{:T(128)S(6)} %add.104), kind=kLoop, calls=%fused_computation.167 | loop fusion | bytes 10485768 | tf_op jit(solution)/shard_map/slice | solution.py:164
  199.5 6.5 copy.116
  209.2 6.0 copy.93
  215.2 8.9 %multiply_convert_fusion.4 = bf16[512,2560]{1,0:T(8,128)(2,1)} fusion(f32[512,2560]{1,0:T(8,128)} %copy.93, bf16[512,2560]{1,0:T(8,128)(2,1)} %bitcast.39, s32[512]{0:T(512)S(1)} %get-tuple-element.15, s32[512]{0:T(512)S(1)} %get-tuple-element.12, s32[512]{0:T(512)S(1)} %get-tuple-element.16, s32[512]{0:T(512)S(1)} %get-tuple-element.11), kind=kOutput, calls=%fused_computation.8 | convolution fusion | flops 2702442496 | bytes 10493952 | tf_op jit(solution)/shard_map/dot_general | solution.py:29
  224.1 22.1 %all-to-all-done = bf16[8,64,2560]{2,1,0:T(8,128)(2,1)} async-done(((bf16[8,64,2560]{2,1,0:T(8,128)(2,1)}), bf16[8,64,2560]{2,1,0:T(8,128)(2,1)}, u32[]{:S(2)}, u32[]{:S(2)}) %all-to-all-start) | async-done | bytes 2621472 | tf_op jit(solution)/shard_map/all_to_all | solution.py:60
  250.4 7.6 copy.117
  258.1 5.6 bitcast_convert_fusion.1
  263.6 6.3 copy.82
  270.0 8.9 %multiply_convert_fusion.10 = bf16[512,2560]{1,0:T(8,128)(2,1)} fusion(f32[512,2560]{1,0:T(8,128)} %copy.82, bf16[512,2560]{1,0:T(8,128)(2,1)} %bitcast.11, s32[512]{0:T(512)S(1)} %get-tuple-element.14, s32[512]{0:T(512)S(1)} %get-tuple-element.15, s32[512]{0:T(512)S(1)} %get-tuple-element.16, s32[512]{0:T(512)S(1)} %get-tuple-element.13), kind=kOutput, calls=%fused_computation.15 | convolution fusion | flops 2702442496 | bytes 10493952 | tf_op jit(solution)/shard_map/dot_general | solution.py:29
  278.9 30.6 %all-to-all-done.6 = bf16[8,64,2560]{2,1,0:T(8,128)(2,1)S(1)} async-done(((bf16[8,64,2560]{2,1,0:T(8,128)(2,1)}), bf16[8,64,2560]{2,1,0:T(8,128)(2,1)S(1)}, u32[]{:S(2)}, u32[]{:S(2)}) %all-to-all-start.6) | async-done | bytes 2621472 | tf_op jit(solution)/shard_map/all_to_all | solution.py:67
  309.5 4.4 all-to-all-start.1
  313.9 14.4 %copy.78 = bf16[4096,1280]{0,1:T(8,128)(2,1)} copy(bf16[4096,1280]{1,0:T(8,128)(2,1)} %param.12) | data formatting | bytes 20971520 | tf_op args[2]
  331.3 8.3 reshape.377
  339.6 4.2 multiply_convert_fusion.3
  345.5 27.4 %all-to-all-done.1 = bf16[8,64,2560]{2,1,0:T(8,128)(2,1)} async-done(((bf16[8,64,2560]{2,1,0:T(8,128)(2,1)}), bf16[8,64,2560]{2,1,0:T(8,128)(2,1)}, u32[]{:S(2)}, u32[]{:S(2)}) %all-to-all-start.1) | async-done | bytes 2621472 | tf_op jit(solution)/shard_map/all_to_all | solution.py:67
  376.8 4.7 dynamic-slice_convert_fusion
  381.5 12.4 %copy.79 = f32[4096,2,1,160]{3,1,0,2:T(2,128)} copy(f32[4096,2,1,160]{0,3,2,1:T(8,128)} %dynamic-slice_convert_fusion) | data formatting | bytes 10485760 | tf_op jit(solution)/shard_map/convert_element_type | solution.py:170
  393.8 10.9 %reshape.388 = f32[64,128,160]{2,1,0:T(8,128)} reshape(f32[4096,2,1,160]{3,1,0,2:T(2,128)} %copy.79) | data formatting | bytes 10485760 | tf_op jit(solution)/shard_map/convert_element_type | solution.py:170
  404.7 8.3 copy.85
  413.1 14.4 %copy.87 = bf16[4096,1280]{0,1:T(8,128)(2,1)} copy(bf16[4096,1280]{1,0:T(8,128)(2,1)} %param.13) | data formatting | bytes 20971520 | tf_op args[3]
  434.5 4.7 copy.83
  439.2 8.3 reshape.362
  447.5 6.2 fusion
  453.8 5.7 copy.86
  459.4 7.3 reshape.364
  466.7 4.8 copy.103
  471.5 10.1 %reshape.380 = bf16[320,4096]{1,0:T(8,128)(2,1)S(1)} reshape(bf16[2,1,8,128,4,160]{5,4,3,2,0,1:T(4,128)(2,1)} %copy.103) | data formatting | bytes 5242880 | tf_op jit(solution)/shard_map/reshape | solution.py:183
  485.2 6.7 convolution_bitcast_fusion.2
  496.4 8.6 fusion.76
  504.9 5.8 reshape_reshape.7
  510.7 5.9 copy.88
  527.4 15.9 %convolution_bitcast_fusion = f32[4096,320]{0,1:T(8,128)} fusion(bf16[1024,4096]{1,0:T(8,128)(2,1)} %all-gather.7.cloned.1.call-done, f32[1024,320]{0,1:T(8,128)} %copy-done.6, bf16[320,4096]{1,0:T(8,128)(2,1)} %bitcast_add_fusion.1, bf16[1024,4096]{1,0:T(8,128)(2,1)} %all-gather.11.cloned.1.call-done, f32[1024,320]{0,1:T(8,128)} %copy-done.7), kind=kOutput, calls=%fused_computation.1 | convolution fusion | flops 5375262720 | bytes 27262976 | tf_op jit(solution)/shard_map/dot_general | solution.py:29
  543.3 6.3 copy.104
  549.6 8.9 %reshape.381 = f32[64,128,160]{2,1,0:T(8,128)} reshape(f32[4096,320]{1,0:T(8,128)} %copy.104) | data formatting | bytes 10485760 | tf_op jit(solution)/shard_map/reshape | solution.py:207
  558.5 6.3 convert_bitcast_fusion
  564.8 5.7 copy.106
  570.5 8.7 reshape.382
  579.2 4.0 copy.107
  583.2 4.6 all-to-all-start.8
  590.0 5.9 copy.91
  595.9 7.7 reshape_reshape.8
  605.9 42.3 %all-to-all-done.8 = bf16[8,64,2560]{2,1,0:T(8,128)(2,1)} async-done(((bf16[8,64,2560]{2,1,0:T(8,128)(2,1)}), bf16[8,64,2560]{2,1,0:T(8,128)(2,1)}, u32[]{:S(2)}, u32[]{:S(2)}) %all-to-all-start.8) | async-done | bytes 2621472 | tf_op jit(solution)/shard_map/all_to_all | solution.py:60
  651.8 8.9 %multiply_convert_fusion.1 = bf16[512,2560]{1,0:T(8,128)(2,1)} fusion(f32[512,2560]{1,0:T(8,128)} %copy.82, bf16[512,2560]{1,0:T(8,128)(2,1)} %bitcast.52, s32[512]{0:T(512)S(1)} %get-tuple-element.14, s32[512]{0:T(512)S(1)} %get-tuple-element.15, s32[512]{0:T(512)S(1)} %get-tuple-element.16, s32[512]{0:T(512)S(1)} %get-tuple-element.13), kind=kOutput, calls=%fused_computation.5 | convolution fusion | flops 2702442496 | bytes 10493952 | tf_op jit(solution)/shard_map/dot_general | solution.py:29
  660.7 50.8 %all-to-all-done.3 = bf16[8,64,2560]{2,1,0:T(8,128)(2,1)S(1)} async-done(((bf16[8,64,2560]{2,1,0:T(8,128)(2,1)}), bf16[8,64,2560]{2,1,0:T(8,128)(2,1)S(1)}, u32[]{:S(2)}, u32[]{:S(2)}) %all-to-all-start.3) | async-done | bytes 2621472 | tf_op jit(solution)/shard_map/all_to_all | solution.py:60
  716.7 9.0 %multiply_convert_fusion.7 = bf16[512,2560]{1,0:T(8,128)(2,1)} fusion(f32[512,2560]{1,0:T(8,128)} %copy.93, bf16[512,2560]{1,0:T(8,128)(2,1)} %bitcast.189, s32[512]{0:T(512)S(1)} %get-tuple-element.15, s32[512]{0:T(512)S(1)} %get-tuple-element.12, s32[512]{0:T(512)S(1)} %get-tuple-element.16, s32[512]{0:T(512)S(1)} %get-tuple-element.11), kind=kOutput, calls=%fused_computation.12 | convolution fusion | flops 2702442496 | bytes 10493952 | tf_op jit(solution)/shard_map/dot_general | solution.py:29
  725.7 50.7 %all-to-all-done.9 = bf16[8,64,2560]{2,1,0:T(8,128)(2,1)S(1)} async-done(((bf16[8,64,2560]{2,1,0:T(8,128)(2,1)}), bf16[8,64,2560]{2,1,0:T(8,128)(2,1)S(1)}, u32[]{:S(2)}, u32[]{:S(2)}) %all-to-all-start.9) | async-done | bytes 2621472 | tf_op jit(solution)/shard_map/all_to_all | solution.py:67
  776.3 4.7 all-to-all-start.4
  784.0 8.3 reshape.385
  792.3 7.3 copy.110
  803.0 37.0 %all-to-all-done.4 = bf16[8,64,2560]{2,1,0:T(8,128)(2,1)} async-done(((bf16[8,64,2560]{2,1,0:T(8,128)(2,1)}), bf16[8,64,2560]{2,1,0:T(8,128)(2,1)}, u32[]{:S(2)}, u32[]{:S(2)}) %all-to-all-start.4) | async-done | bytes 2621472 | tf_op jit(solution)/shard_map/all_to_all | solution.py:67
  843.2 6.2 reshape.370
  849.4 7.3 copy.95
  860.2 10.9 %psum.7 = f32[64,128]{1,0:T(8,128)} all-reduce(f32[64,128]{1,0:T(8,128)S(1)} %add_multiply_fusion), channel_id=1, replica_groups=mesh['dp'=4,'fsdp'=8] {'dp'}, use_global_device_ids=true, to_apply=%region_2.3 | all-reduce | flops 8192 | bytes 65536 | tf_op jit(solution)/shard_map/psum | solution.py:218
  (63 shorter events, 80.9 us)
Async XLA Ops:
  6.5 55.0 %all-gather.5.cloned.1.call-start = ((), (), s32[]{:S(2)}) async-start(), calls=%async_computation.10 | async-start | bytes 2359296 | tf_op jit(solution)/shard_map/all_gather | solution.py:143
  7.3 242.8 %all-gather.9.cloned.1.call-start = ((), (), s32[]{:S(2)}) async-start(), calls=%async_computation.12 | async-start | bytes 2359296 | tf_op jit(solution)/shard_map/all_gather | solution.py:144
  8.0 477.1 %all-gather.7.cloned.1.call-start = ((), (), s32[]{:S(2)}) async-start(), calls=%async_computation.11 | async-start | bytes 10485760 | tf_op jit(solution)/shard_map/all_gather | solution.py:143
  91.5 7.8 copy-start.3
  119.4 63.4 %all-to-all-start.5 = ((bf16[8,64,2560]{2,1,0:T(8,128)(2,1)}), bf16[8,64,2560]{2,1,0:T(8,128)(2,1)}, u32[]{:S(2)}, u32[]{:S(2)}) async-start(bf16[8,64,2560]{2,1,0:T(8,128)(2,1)} %copy.98), calls=%async_computation.5 | async-start | bytes 5242880 | tf_op jit(solution)/shard_map/all_to_all | solution.py:60
  182.8 63.4 %all-to-all-start = ((bf16[8,64,2560]{2,1,0:T(8,128)(2,1)}), bf16[8,64,2560]{2,1,0:T(8,128)(2,1)}, u32[]{:S(2)}, u32[]{:S(2)}) async-start(bf16[8,64,2560]{2,1,0:T(8,128)(2,1)} %copy.81), calls=%async_computation | async-start | bytes 5242880 | tf_op jit(solution)/shard_map/all_to_all | solution.py:60
  209.2 6.0 copy-start.4
  246.2 63.3 %all-to-all-start.6 = ((bf16[8,64,2560]{2,1,0:T(8,128)(2,1)}), bf16[8,64,2560]{2,1,0:T(8,128)(2,1)S(1)}, u32[]{:S(2)}, u32[]{:S(2)}) async-start(bf16[8,64,2560]{2,1,0:T(8,128)(2,1)} %bitcast.187), calls=%async_computation.6 | async-start | bytes 5242880 | tf_op jit(solution)/shard_map/all_to_all | solution.py:67
  249.9 246.5 %all-gather.11.cloned.1.call-start = ((), (), s32[]{:S(2)}) async-start(), calls=%async_computation.13 | async-start | bytes 10485760 | tf_op jit(solution)/shard_map/all_gather | solution.py:144
  309.5 63.4 %all-to-all-start.1 = ((bf16[8,64,2560]{2,1,0:T(8,128)(2,1)}), bf16[8,64,2560]{2,1,0:T(8,128)(2,1)}, u32[]{:S(2)}, u32[]{:S(2)}) async-start(bf16[8,64,2560]{2,1,0:T(8,128)(2,1)} %bitcast.188), calls=%async_computation.1 | async-start | bytes 5242880 | tf_op jit(solution)/shard_map/all_to_all | solution.py:67
  313.9 14.4 %copy-start.2 = (f32[2,64,640]{2,1,0:T(8,128)S(1)}, f32[2,64,640]{2,1,0:T(8,128)}, u32[]{:S(2)}) copy-start(f32[2,64,640]{2,1,0:T(8,128)} %param.18) | copy-start | bytes 983044
  372.9 93.8 %all-to-all-start.7 = ((bf16[2,4,8,128,160]{3,4,2,0,1:T(8,128)(2,1)}), bf16[2,4,8,128,160]{3,4,2,0,1:T(8,128)(2,1)S(1)}, u32[]{:S(2)}, u32[]{:S(2)}) async-start(bf16[2,4,8,128,160]{3,4,2,0,1:T(8,128)(2,1)} %copy.102), calls=%async_computation.7 | async-start | bytes 5242880 | tf_op jit(solution)/shard_map/all_to_all | solution.py:179
  413.1 14.4 %slice-start = ((f32[2,64,640]{2,1,0:T(8,128)}), f32[1,64,640]{2,1,0:T(8,128)S(1)}, s32[]{:S(2)}) async-start(f32[2,64,640]{2,1,0:T(8,128)} %param.18), calls=%async_computation.14 | async-start | bytes 327680 | tf_op jit(solution)/shard_map/slice | solution.py:194
  485.1 6.7 copy-start
  485.2 7.5 copy-start.5
  492.7 3.7 copy-start.6
  496.3 8.6 copy-start.7
  523.6 59.6 %all-to-all-start.2 = ((bf16[2,1,8,128,640]{3,2,0,1,4:T(8,128)(2,1)}), bf16[2,1,8,128,640]{3,2,0,1,4:T(8,128)(2,1)S(1)}, u32[]{:S(2)}, u32[]{:S(2)}) async-start(bf16[2,1,8,128,640]{3,2,0,1,4:T(8,128)(2,1)} %copy.89), calls=%async_computation.2 | async-start | bytes 5242880 | tf_op jit(solution)/shard_map/all_to_all | solution.py:201
  583.2 65.0 %all-to-all-start.8 = ((bf16[8,64,2560]{2,1,0:T(8,128)(2,1)}), bf16[8,64,2560]{2,1,0:T(8,128)(2,1)}, u32[]{:S(2)}, u32[]{:S(2)}) async-start(bf16[8,64,2560]{2,1,0:T(8,128)(2,1)} %copy.107), calls=%async_computation.8 | async-start | bytes 5242880 | tf_op jit(solution)/shard_map/all_to_all | solution.py:60
  648.2 63.3 %all-to-all-start.3 = ((bf16[8,64,2560]{2,1,0:T(8,128)(2,1)}), bf16[8,64,2560]{2,1,0:T(8,128)(2,1)S(1)}, u32[]{:S(2)}, u32[]{:S(2)}) async-start(bf16[8,64,2560]{2,1,0:T(8,128)(2,1)} %copy.92), calls=%async_computation.3 | async-start | bytes 5242880 | tf_op jit(solution)/shard_map/all_to_all | solution.py:60
  711.6 1.5 copy-start.1
  713.1 63.3 %all-to-all-start.9 = ((bf16[8,64,2560]{2,1,0:T(8,128)(2,1)}), bf16[8,64,2560]{2,1,0:T(8,128)(2,1)S(1)}, u32[]{:S(2)}, u32[]{:S(2)}) async-start(bf16[8,64,2560]{2,1,0:T(8,128)(2,1)} %bitcast.191), calls=%async_computation.9 | async-start | bytes 5242880 | tf_op jit(solution)/shard_map/all_to_all | solution.py:67
  776.3 63.7 %all-to-all-start.4 = ((bf16[8,64,2560]{2,1,0:T(8,128)(2,1)}), bf16[8,64,2560]{2,1,0:T(8,128)(2,1)}, u32[]{:S(2)}, u32[]{:S(2)}) async-start(bf16[8,64,2560]{2,1,0:T(8,128)(2,1)} %bitcast.190), calls=%async_computation.4 | async-start | bytes 5242880 | tf_op jit(solution)/shard_map/all_to_all | solution.py:67
Sparse Core Ops, SparseCore 0:
  9.5 51.9 all-gather.4
  63.6 47.7 all-gather.8
  113.0 56.7 all-gather.6
  252.0 58.7 all-gather.10

commit v2 on v1

v2 whole, which is shorter than its diff:
```python
import functools

import jax
import jax.numpy as jnp
from jax import lax
from jax.experimental import pallas as pl
from jax.experimental.pallas import tpu as pltpu
from jax.sharding import PartitionSpec as P

D = 4096
FF = 10240


def hadamard(size, dtype):
    index = jnp.arange(size, dtype=jnp.int32)
    anded = jnp.bitwise_and(index[:, None], index[None, :])
    parity = jnp.zeros((size, size), jnp.int32)
    for bit in range(max(size.bit_length() - 1, 0)):
        parity = jnp.bitwise_xor(parity, jnp.bitwise_and(jnp.right_shift(anded, bit), 1))
    return (1 - 2 * parity).astype(dtype)


def gelu_pair(value):
    argument = 0.7978845608028654 * (value + 0.044715 * value * value * value)
    tangent = jnp.tanh(argument)
    slope = 0.5 * (1.0 + tangent) + 0.5 * value * (1.0 - tangent * tangent) * 0.7978845608028654 * (
        1.0 + 0.134145 * value * value
    )
    return 0.5 * value * (1.0 + tangent), slope


def contract(left, right, left_dim, right_dim):
    return lax.dot_general(
        left, right, (((left_dim,), (right_dim,)), ((), ())), preferred_element_type=jnp.float32
    )


def hadamard_rows(order, size):
    anded = jnp.bitwise_and(order[:, None], jnp.arange(size, dtype=jnp.int32)[None, :])
    parity = jnp.zeros(anded.shape, jnp.int32)
    for bit in range(max(size.bit_length() - 1, 0)):
        parity = jnp.bitwise_xor(parity, jnp.bitwise_and(jnp.right_shift(anded, bit), 1))
    return (1 - 2 * parity).astype(jnp.bfloat16)


def forward_kernel(some, scale_in, scale_out, s_ref, g_ref, sub_ref, rows_ref, tall_ref, wide_ref, e_ref, u_ref):
    width = wide_ref.shape[0]
    sub = sub_ref[...]
    for at in range(some):
        lifted = s_ref[:, at * width : (at + 1) * width] * sub
        u_ref[at * width : (at + 1) * width, :] = contract(wide_ref[...], lifted, 1, 1).astype(
            jnp.bfloat16
        )
    turned = contract(u_ref[...], rows_ref[...], 1, 1) * scale_in
    mixed = (g_ref[...].astype(jnp.float32) * turned).astype(jnp.bfloat16)
    u_ref[...] = contract(mixed, tall_ref[...], 1, 0).astype(jnp.bfloat16)
    for at in range(some):
        wide = contract(u_ref[at * width : (at + 1) * width, :], wide_ref[...], 0, 0)
        e_ref[:, at * width : (at + 1) * width] = (wide * scale_out).astype(jnp.bfloat16)


def adjoint_kernel(some, scale_out, b_ref, s_ref, g_ref, rows_ref, tall_ref, wide_ref, sum_ref, u_ref):
    width = wide_ref.shape[0]

    @pl.when(pl.program_id(0) == 0)
    def _():
        sum_ref[...] = jnp.zeros_like(sum_ref)

    for at in range(some):
        u_ref[at * width : (at + 1) * width, :] = contract(
            wide_ref[...], b_ref[:, at * width : (at + 1) * width], 1, 1
        ).astype(jnp.bfloat16)
    spread = contract(u_ref[...], tall_ref[...], 1, 0)
    spread = (g_ref[...].astype(jnp.float32) * spread).astype(jnp.bfloat16)
    u_ref[...] = contract(spread, rows_ref[...], 1, 0).astype(jnp.bfloat16)
    total = jnp.zeros(sum_ref.shape, jnp.float32)
    for at in range(some):
        wide = contract(u_ref[at * width : (at + 1) * width, :], wide_ref[...], 0, 0)
        total += s_ref[:, at * width : (at + 1) * width].astype(jnp.float32) * wide
    sum_ref[...] += total * scale_out


def vectors_at_once(count):
    return max(some for some in range(1, 6) if count % some == 0)


def chain(kernel, operands, whole, result, width, blocks_all, count, summed):
    some = vectors_at_once(count)
    flat = pl.BlockSpec((blocks_all, some * width), lambda i: (0, i))
    turned = pl.BlockSpec((some * width, blocks_all), lambda i: (i, 0))
    specs = [flat if item.shape[0] == blocks_all else turned for item in operands]
    specs += [pl.BlockSpec(item.shape, lambda i: (0, 0)) for item in whole]
    flops = 2 * count * width * blocks_all * (2 * blocks_all + 2 * width)
    return pl.pallas_call(
        functools.partial(kernel, some),
        grid=(count // some,),
        in_specs=specs,
        out_specs=pl.BlockSpec((blocks_all, width), lambda i: (0, 0)) if summed else flat,
        out_shape=result,
        scratch_shapes=[pltpu.VMEM((some * width, blocks_all), jnp.bfloat16)],
        compiler_params=pltpu.CompilerParams(vmem_limit_bytes=40 * 1024 * 1024),
        cost_estimate=pl.CostEstimate(
            flops=flops, bytes_accessed=6 * count * width * blocks_all, transcendentals=0
        ),
    )(*operands, *whole)


def exchange(item):
    return lax.all_to_all(item, "fsdp", split_axis=0, concat_axis=0, tiled=True)


def on_device(
    tokens,
    cotangent,
    gate_base,
    up_base,
    out_base,
    subspace,
    sign_flips,
    fast_gains,
    fast_scales,
    block_orders,
):
    parts, groups = lax.axis_size("fsdp"), lax.axis_size("dp")
    mine = lax.axis_index("dp")
    _, inner, width, vectors = sign_flips.shape
    blocks_all, some = fast_gains.shape[1], fast_gains.shape[2]
    share = vectors // groups
    hidden_here = gate_base.shape[1]
    direct = hidden_here % vectors == 0
    runs = hidden_here // vectors if direct else 1
    piece = hidden_here // (runs * groups)
    owned = runs * piece

    factors = (D ** (-0.5), FF ** (-0.5))
    slab = (inner, width, vectors)

    def k_slice(item):
        return lax.dynamic_slice_in_dim(item, mine * share, share, axis=item.ndim - 1)

    def hidden_columns(item):
        cut = item.reshape(item.shape[0], runs, groups, piece)
        cut = lax.dynamic_index_in_dim(cut, mine, 2, keepdims=False)
        return cut.reshape(item.shape[0], owned)

    count = -(-share // parts)
    wide_h, tall_h = hadamard(width, jnp.bfloat16), hadamard(blocks_all, jnp.bfloat16)
    rows_h = [hadamard_rows(block_orders[which], blocks_all) for which in range(2)]
    sub_all = lax.all_gather(subspace.astype(jnp.bfloat16), "fsdp", axis=0, tiled=True)

    def filled(item):
        if count * parts == share:
            return item
        return jnp.pad(item, ((0, 0), (0, 0), (0, count * parts - share)))

    def signs_to_owners(which):
        item = filled(k_slice(sign_flips[which]).astype(jnp.bfloat16))
        item = item.reshape(inner, width, parts, count).transpose(2, 0, 3, 1)
        return exchange(item.reshape(parts, inner, count * width)).reshape(blocks_all, count * width)

    def gains_to_owners(which):
        item = filled(k_slice(fast_gains[which])).reshape(blocks_all, some, parts, count)
        item = exchange(item.transpose(2, 3, 1, 0))
        return item.transpose(1, 0, 2, 3).reshape(count * width, blocks_all)

    def weights_home(item):
        item = exchange(item.reshape(parts, inner, count * width))
        item = item.reshape(parts, inner, count, width).transpose(1, 3, 0, 2)
        return item.reshape(inner, width, parts * count)[:, :, :share]

    def grads_to_owners(item):
        item = filled(item).reshape(inner, width, parts, count).transpose(2, 0, 3, 1)
        return exchange(item.reshape(parts, inner, count * width)).reshape(blocks_all, count * width)

    def expand(which):
        return chain(
            lambda some, *refs: forward_kernel(
                some,
                (blocks_all * width) ** (-0.5),
                (blocks_all * width) ** (-0.5),
                *refs,
            ),
            (signs[which], gains[which]),
            (sub_all, rows_h[which], tall_h, wide_h),
            jax.ShapeDtypeStruct((blocks_all, count * width), jnp.bfloat16),
            width,
            blocks_all,
            count,
            False,
        )

    gains_0 = gains_to_owners(0)
    signs_0 = signs_to_owners(0)
    gains_1 = gains_to_owners(1)
    signs_1 = signs_to_owners(1)
    signs, gains = (signs_0, signs_1), (gains_0, gains_1)

    x = lax.all_gather(tokens, "fsdp", axis=0, tiled=True)
    dy = lax.all_gather(cotangent, "fsdp", axis=0, tiled=True)
    x, dy, sub_all, gains_0 = lax.optimization_barrier((x, dy, sub_all, gains_0))
    gains = (gains_0, gains_1)
    x = lax.all_gather(x, "dp", axis=0, tiled=True)
    dy = lax.all_gather(dy, "dp", axis=0, tiled=True)

    def scaled_home(which):
        own = k_slice(fast_scales[which])[:, None, :] * factors[which]
        return weights_home(expand(which)).astype(jnp.float32) * own

    delta_gate = scaled_home(0)
    if direct:
        base_gate = hidden_columns(gate_base).reshape(inner, width, share)
        gate_weight = (base_gate + delta_gate).astype(jnp.bfloat16).reshape(D, owned)
    else:
        base_gate = k_slice(gate_base.reshape(slab))
        gate_weight = (base_gate + delta_gate).astype(jnp.bfloat16)
        gate_weight = lax.all_gather(gate_weight, "dp", axis=2, tiled=True)
        gate_weight = hidden_columns(gate_weight.reshape(gate_base.shape))

    strip = inner // (runs * groups)
    delta_out = scaled_home(1).astype(jnp.bfloat16).reshape(runs, groups, strip, width, share)
    delta_out = lax.all_to_all(delta_out, "dp", split_axis=1, concat_axis=4, tiled=True)
    base_out = lax.dynamic_index_in_dim(
        out_base.reshape(runs, groups, piece, D), mine, 1, keepdims=False
    )
    out_weight = base_out.reshape(owned, D) + delta_out.reshape(owned, D)

    gate = jnp.dot(x, gate_weight, preferred_element_type=jnp.float32)
    up = jnp.dot(x, hidden_columns(up_base), preferred_element_type=jnp.float32)
    bent, slope = gelu_pair(gate)
    hidden = (bent * up).astype(jnp.bfloat16)
    hidden_grad = contract(dy, out_weight, 1, 1)
    gate_grad = (hidden_grad * up * slope).astype(jnp.bfloat16)

    out_grad = contract(hidden, dy, 0, 0).reshape(runs, strip, width, vectors)
    back_factor = (blocks_all * width) ** (-0.5)
    strips = lax.dynamic_index_in_dim(
        fast_scales[1].reshape(runs, groups, strip, vectors), mine, 1, keepdims=False
    )
    back_out = (out_grad * (strips[:, :, None, :] * (factors[1] * back_factor))).astype(jnp.bfloat16)
    back_out = lax.all_to_all(
        back_out.reshape(runs, 1, strip, width, vectors), "dp", split_axis=4, concat_axis=1, tiled=True
    ).reshape(inner, width, share)

    in_grad = contract(x, gate_grad, 0, 0)
    if direct:
        in_grad = in_grad.reshape(inner, width, share)
    else:
        in_grad = lax.all_gather(in_grad.astype(jnp.bfloat16), "dp", axis=1, tiled=True)
        in_grad = k_slice(in_grad.reshape(slab)).astype(jnp.float32)
    own = k_slice(fast_scales[0])[:, None, :] * (factors[0] * back_factor)
    back_gate = (in_grad * own).astype(jnp.bfloat16)

    def fold(back, which):
        return chain(
            lambda some, *refs: adjoint_kernel(some, (blocks_all * width) ** (-0.5), *refs),
            (grads_to_owners(back), signs[which], gains[which]),
            (rows_h[which], tall_h, wide_h),
            jax.ShapeDtypeStruct((blocks_all, width), jnp.float32),
            width,
            blocks_all,
            count,
            True,
        )

    result = fold(back_out, 1) + fold(back_gate, 0)
    result = lax.psum_scatter(result, "fsdp", scatter_dimension=0, tiled=True)
    return lax.psum(result, "dp")


def solution(mesh):
    in_specs = (
        P(("dp", "fsdp"), None),
        P(("dp", "fsdp"), None),
        P(None, "fsdp"),
        P(None, "fsdp"),
        P("fsdp", None),
        P("fsdp", None),
        P(None, "fsdp", None, None),
        P(None, None, "fsdp", None),
        P(None, "fsdp", None),
        P(),
    )
    out_specs = P("fsdp", None)
    return jax.shard_map(
        on_device, mesh=mesh, in_specs=in_specs, out_specs=out_specs, check_vma=False
    )
```

time: 889 us -> 989 us (1.11)
  blocking collectives: 10.9 us -> 105 us
  matrix products: 105 us -> 43.8 us
  Pallas kernels: 0 us -> 25.4 us
  other arithmetic: 24.9 us -> 41.4 us
  local copies, waits for them, and re-layouts: 327 us -> 340 us
    all_gather x0 -> x1, blocking collectives: none -> 93.5 us  [on_device(): lax.all_gather(subspace.astype(jnp.bfloat16), 'fsdp', axis=0, tiled=True)]
    reduce_scatter x0 -> x1, waiting for transfers between devices: none -> 60.2 us  [on_device(): result = lax.psum_scatter(result, 'fsdp', scatter_dimension=0, tiled=True)]
    reshape x12 -> x6, local copies, waits for them, and re-layouts: 82 us -> 23.4 us  [the longest x2 12 us: on_device(): out_grad = contract(hidden, dy, 0, 0).reshape(runs, strip, width, vectors)]
    all_gather x4, waiting for transfers between devices: 53.5 us -> 0.01 us  [the longest x1 0.01 us: on_device(): x = lax.all_gather(tokens, 'fsdp', axis=0, tiled=True)]
    dot_general x8 -> x0, matrix products: 34.1 us -> none  [the longest x2 10.4 us: local_finish(): jnp.einsum('dc,ack->adk', hadamard(width, jnp.bfloat16), second, preferre...]
    slice x1 -> x2, local copies, waits for them, and re-layouts: 12.3 us -> 46.3 us  [the longest x1 29.2 us: signs_to_owners(): item = filled(k_slice(sign_flips[which]).astype(jnp.bfloat16))]
    dot_general x6 -> x2, matrix products: 60.1 us -> 27.4 us  [contract(): lax.dot_general(left, right, (((left_dim,), (right_dim,)), ((), ())), pre...]
    pallas_call x0 -> x4, Pallas kernels: none -> 25.4 us  [chain(): pl.pallas_call(functools.partial(kernel, some), grid=(count // some,), in...]
  transfers between devices with their start and end apart: 14 -> 15, of which waited for: 9 -> 8; matrix products, arithmetic and copies ran while one was open for 46% -> 35% of each run, Pallas kernels for 0% -> 2%
where the time goes in v2:
time: 989 us; the launch traced here: 975 us
  waiting for transfers between devices  358 us (36%)
  local copies, waits for them, and re-layouts  340 us (34%)
  blocking collectives  105 us (11%)
  starting transfers between devices  47.8 us (5%)
  matrix products  43.8 us (4%)
  other arithmetic  41.4 us (4%)
  Pallas kernels  25.4 us (3%)
  between operations  14 us (1%)
    all_to_all x8, waiting for transfers between devices, exchange(): return lax.all_to_all(item, 'fsdp', split_axis=0, concat_axis=0, tiled=True)  296 us
    all_gather x1, blocking collectives, on_device(): lax.all_gather(subspace.astype(jnp.bfloat16), 'fsdp', axis=0, tiled=True)  93.5 us
    unnamed x53, local copies, waits for them, and re-layouts  77.5 us
    convert_element_type x6, local copies, waits for them, and re-layouts, scaled_home(): return weights_home(expand(which)).astype(jnp.float32) * own  65.3 us
    reduce_scatter x1, waiting for transfers between devices, on_device(): result = lax.psum_scatter(result, 'fsdp', scatter_dimension=0, tiled=True)  60.2 us
    all_to_all x8, starting transfers between devices, exchange(): return lax.all_to_all(item, 'fsdp', split_axis=0, concat_axis=0, tiled=True)  38.1 us
    slice x1, local copies, waits for them, and re-layouts, signs_to_owners(): item = filled(k_slice(sign_flips[which]).astype(jnp.bfloat16))  29.2 us
    dot_general x2, matrix products, contract(): lax.dot_general(left, right, (((left_dim,), (right_dim,)), ((), ())), pre...  27.4 us
  transfers between devices with their start and end apart: 15, of which 8 were waited for; matrix products, arithmetic and copies ran while one was open for 35% of the time, Pallas kernels for 2%

profile of v2, /device:TPU:0, one launch (start us, length us, event | category | flops | bytes accessed | tf_op | source)
XLA Modules:
  0.0 975.3 jit_solution(12145981695024688213)
XLA Ops:
  7.3 17.2 %fusion.21 = (bf16[1,512,16,640]{3,2,1,0:T(8,128)(2,1)}, bf16[1,512,16,640]{3,2,1,0:T(8,128)(2,1)}) fusion(bf16[2,512,16,640]{3,2,1,0:T(8,128)(2,1)} %param.17), kind=kLoop, calls=%fused_computation.47 | loop fusion | bytes 41943040 | tf_op jit(solution)/shard_map/slice | solution.py:162
  24.4 12.3 %constant_dynamic-slice_fusion.1 = (bf16[1,512,16,160]{3,2,1,0:T(8,128)(2,1)}, bf16[1,512,16,160]{3,2,1,0:T(8,128)(2,1)}) fusion(bf16[1,512,16,640]{3,2,1,0:T(8,128)(2,1)} %get-tuple-element.15, s32[]{:T(128)S(6)} %select_n.10, bf16[1,512,16,640]{3,2,1,0:T(8,128)(2,1)} %get-tuple-element.16), kind=kLoop, calls=%fused_computation.36 | loop fusion | bytes 10485764 | tf_op jit(solution)/shard_map/dynamic_slice | solution.py:139
  36.7 8.2 copy.69
  44.9 7.4 all-to-all-start
  53.0 29.2 %fusion.20 = (s32[1,64,128,640]{3,2,1,0:T(8,128)}, s32[1,64,128,640]{3,2,1,0:T(8,128)}) fusion(s32[2,64,128,640]{3,2,1,0:T(8,128)} %param.16), kind=kLoop, calls=%fused_computation.46 | loop fusion | bytes 83886080 | tf_op jit(solution)/shard_map/slice | solution.py:157
  82.2 15.0 %constant_dynamic-slice_fusion.2 = (s32[1,64,128,160]{3,2,1,0:T(8,128)}, s32[1,64,128,160]{3,2,1,0:T(8,128)}) fusion(s32[1,64,128,640]{3,2,1,0:T(8,128)} %get-tuple-element.13, s32[]{:T(128)S(6)} %select_n.10, s32[1,64,128,640]{3,2,1,0:T(8,128)} %get-tuple-element.14), kind=kLoop, calls=%fused_computation.37 | loop fusion | bytes 20971524 | tf_op jit(solution)/shard_map/dynamic_slice | solution.py:139
  97.2 8.0 copy.74
  105.2 3.2 convert_element_type.117
  110.4 15.3 %all-to-all-done = bf16[8,20,16,512]{3,2,1,0:T(8,128)(2,1)S(1)} async-done(((bf16[8,20,16,512]{3,2,1,0:T(8,128)(2,1)}), bf16[8,20,16,512]{3,2,1,0:T(8,128)(2,1)S(1)}, u32[]{:S(2)}, u32[]{:S(2)}) %all-to-all-start) | async-done | bytes 2621472 | tf_op jit(solution)/shard_map/all_to_all | solution.py:109
  127.2 3.6 all-to-all-start.5
  130.9 93.5 %all_gather.17.refs_2_ = bf16[512,128]{1,0:T(8,128)(2,1)S(1)} all-gather(bf16[64,128]{1,0:T(8,128)(2,1)S(1)} %convert_element_type.102), channel_id=1, replica_groups=mesh['dp'=4,'fsdp'=8] {'fsdp'}, dimensions={0}, use_global_device_ids=true | all-gather | bytes 147456 | tf_op jit(solution)/shard_map/all_gather | solution.py:149
  224.4 3.5 copy.41
  228.0 8.3 copy.76
  236.2 4.6 all-to-all-start.6
  240.9 8.0 copy.71
  248.9 3.2 convert_element_type.105
  254.0 41.6 %all-to-all-done.6 = bf16[8,20,16,512]{3,2,1,0:T(8,128)(2,1)} async-done(((bf16[8,20,16,512]{3,2,1,0:T(8,128)(2,1)}), bf16[8,20,16,512]{3,2,1,0:T(8,128)(2,1)}, u32[]{:S(2)}, u32[]{:S(2)}) %all-to-all-start.6) | async-done | bytes 2621472 | tf_op jit(solution)/shard_map/all_to_all | solution.py:109
  295.6 4.6 all-to-all-start.1
  301.4 3.0 subtract_convert_fusion.1
  306.7 5.7 shard_map.102
  315.4 43.5 %all-to-all-done.1 = bf16[8,64,2560]{2,1,0:T(8,128)(2,1)} async-done(((bf16[8,64,2560]{2,1,0:T(8,128)(2,1)}), bf16[8,64,2560]{2,1,0:T(8,128)(2,1)}, u32[]{:S(2)}, u32[]{:S(2)}) %all-to-all-start.1) | async-done | bytes 2621472 | tf_op jit(solution)/shard_map/all_to_all | solution.py:109
  359.0 4.4 all-to-all-start.7
  366.8 6.5 shard_map.100
  374.8 47.6 %all-to-all-done.7 = bf16[8,64,2560]{2,1,0:T(8,128)(2,1)} async-done(((bf16[8,64,2560]{2,1,0:T(8,128)(2,1)}), bf16[8,64,2560]{2,1,0:T(8,128)(2,1)}, u32[]{:S(2)}, u32[]{:S(2)}) %all-to-all-start.7) | async-done | bytes 2621472 | tf_op jit(solution)/shard_map/all_to_all | solution.py:109
  422.4 4.5 all-to-all-start.2
  428.0 5.9 reshape.192
  434.0 3.7 copy.59
  441.4 44.5 %all-to-all-done.2 = bf16[8,64,2560]{2,1,0:T(8,128)(2,1)} async-done(((bf16[8,64,2560]{2,1,0:T(8,128)(2,1)}), bf16[8,64,2560]{2,1,0:T(8,128)(2,1)}, u32[]{:S(2)}, u32[]{:S(2)}) %all-to-all-start.2) | async-done | bytes 2621472 | tf_op jit(solution)/shard_map/all_to_all | solution.py:109
  485.9 4.9 all-to-all-start.8
  490.9 4.0 mul.195
  494.8 9.2 mul.196
  504.0 6.3 copy.47
  510.3 14.3 %copy.48 = bf16[4096,1280]{0,1:T(8,128)(2,1)} copy(bf16[4096,1280]{1,0:T(8,128)(2,1)} %param.13) | data formatting | bytes 20971520 | tf_op args[3]
  524.6 14.4 %copy.42 = bf16[4096,1280]{0,1:T(8,128)(2,1)} copy(bf16[4096,1280]{1,0:T(8,128)(2,1)} %param.12) | data formatting | bytes 20971520 | tf_op args[2]
  541.5 3.5 constant_dynamic-slice_fusion
  545.1 5.6 constant_dynamic-slice_fusion.3
  550.7 5.9 reshape.191
  556.6 17.6 %copy.45 = f32[64,128,8,20]{3,2,1,0:T(8,128)} copy(f32[64,128,8,20]{1,3,0,2:T(8,128)} %bitcast.93) | data formatting | bytes 10485760 | tf_op jit(solution)/shard_map/convert_element_type | solution.py:207
  574.2 25.8 %reshape.189 = f32[4096,320]{1,0:T(8,128)} reshape(f32[64,128,8,20]{3,2,1,0:T(8,128)} %copy.45) | data formatting | bytes 10485760 | tf_op jit(solution)/shard_map/convert_element_type | solution.py:207
  600.0 6.3 copy.46
  606.3 6.4 copy.62
  612.7 11.1 %reshape.184 = bf16[320,4096]{1,0:T(8,128)(2,1)} reshape(bf16[2,1,8,128,4,160]{5,4,3,2,0,1:T(4,128)(2,1)} %copy.62) | data formatting | bytes 5242880 | tf_op jit(solution)/shard_map/reshape | solution.py:225
  623.8 4.3 bitcast_add_fusion
  628.1 8.3 fusion.24
  636.4 8.1 fusion.2
  644.5 17.9 %fusion.25 = f32[4096,320]{1,0:T(8,128)} fusion(bf16[1024,4096]{1,0:T(8,128)(2,1)} %all-gather.9.cloned.1.call-done, f32[1024,320]{0,1:T(8,128)} %fusion.24, bf16[1024,4096]{1,0:T(8,128)(2,1)} %all-gather.11.cloned.1.call-done, bf16[320,4096]{1,0:T(8,128)(2,1)} %bitcast_add_fusion, f32[1024,320]{0,1:T(8,128)} %fusion.2), kind=kOutput, calls=%fused_computation.51 | convolution fusion | flops 5375262720 | bytes 27262976 | tf_op jit(solution)/shard_map/dot_general | solution.py:33
  662.4 24.6 %reshape.185 = f32[64,128,8,20]{3,2,1,0:T(8,128)} reshape(f32[4096,320]{1,0:T(8,128)} %fusion.25) | data formatting | bytes 10485760 | tf_op jit(solution)/shard_map/reshape | solution.py:246
  687.0 9.5 fusion.11
  696.5 5.8 reshape.174
  702.3 6.2 copy.50
  708.5 4.3 multiply_convert_fusion.2
  712.8 4.5 all-to-all-start.3
  717.4 17.6 %fusion = bf16[8,64,20,128]{2,0,3,1:T(8,128)(2,1)} fusion(f32[64,128,8,20]{3,2,1,0:T(8,128)} %reshape.185, f32[64,8,20]{2,1,0:T(8,128)S(1)} %reshape.193), kind=kLoop, calls=%fused_computation.1 | loop fusion | flops 2621440 | bytes 7905280 | tf_op jit(solution)/shard_map/transpose | solution.py:172
  735.0 17.2 %copy.66 = bf16[8,64,20,128]{3,2,1,0:T(8,128)(2,1)} copy(bf16[8,64,20,128]{2,0,3,1:T(8,128)(2,1)} %fusion) | data formatting | bytes 5242880 | tf_op jit(solution)/shard_map/transpose | solution.py:172
  752.2 5.6 reshape.186
  757.8 4.4 all-to-all-start.9
  762.2 2.4 copy.51
  768.3 54.3 %all-to-all-done.9 = bf16[8,64,2560]{2,1,0:T(8,128)(2,1)} async-done(((bf16[8,64,2560]{2,1,0:T(8,128)(2,1)}), bf16[8,64,2560]{2,1,0:T(8,128)(2,1)}, u32[]{:S(2)}, u32[]{:S(2)}) %all-to-all-start.9) | async-done | bytes 2621472 | tf_op jit(solution)/shard_map/all_to_all | solution.py:109
  822.6 4.6 all-to-all-start.4
  831.0 6.7 shard_map.103
  837.7 49.0 %all-to-all-done.4 = bf16[8,64,2560]{2,1,0:T(8,128)(2,1)} async-done(((bf16[8,64,2560]{2,1,0:T(8,128)(2,1)}), bf16[8,64,2560]{2,1,0:T(8,128)(2,1)}, u32[]{:S(2)}, u32[]{:S(2)}) %all-to-all-start.4) | async-done | bytes 2621472 | tf_op jit(solution)/shard_map/all_to_all | solution.py:109
  889.5 6.4 shard_map.101
  896.7 60.2 %reduce-scatter.2.cloned.1.call-done = f32[64,128]{1,0:T(8,128)} async-done(((f32[512,128]{1,0:T(8,128)}), f32[64,128]{1,0:T(8,128)}) %reduce-scatter.2.cloned.1.call-update) | async-done | bytes 32784 | tf_op jit(solution)/shard_map/reduce_scatter | solution.py:266
  956.9 11.4 %psum.7 = f32[64,128]{1,0:T(8,128)} all-reduce(f32[64,128]{1,0:T(8,128)} %reduce-scatter.2.cloned.1.call-done), channel_id=1, replica_groups=mesh['dp'=4,'fsdp'=8] {'dp'}, use_global_device_ids=true, to_apply=%region_1.2 | all-reduce | flops 8192 | bytes 65536 | tf_op jit(solution)/shard_map/psum | solution.py:267
  (81 shorter events, 36.7 us)
Async XLA Ops:
  6.5 221.4 %all-gather.5.cloned.1.call-start = ((), (), s32[]{:S(2)}) async-start(), calls=%async_computation.11 | async-start | bytes 2359296 | tf_op jit(solution)/shard_map/all_gather | solution.py:198
  44.9 80.8 %all-to-all-start = ((bf16[8,20,16,512]{3,2,1,0:T(8,128)(2,1)}), bf16[8,20,16,512]{3,2,1,0:T(8,128)(2,1)S(1)}, u32[]{:S(2)}, u32[]{:S(2)}) async-start(bf16[8,20,16,512]{3,2,1,0:T(8,128)(2,1)} %bitcast.100), calls=%async_computation | async-start | bytes 5242880 | tf_op jit(solution)/shard_map/all_to_all | solution.py:109
  52.3 175.6 %all-gather.7.cloned.1.call-start = ((), (), s32[]{:S(2)}) async-start(), calls=%async_computation.12 | async-start | bytes 2359296 | tf_op jit(solution)/shard_map/all_gather | solution.py:199
  125.7 1.5 copy-start.15
  125.7 5.1 copy-start.21
  127.2 109.0 %all-to-all-start.5 = ((bf16[8,64,2560]{2,1,0:T(8,128)(2,1)}), bf16[8,64,2560]{2,1,0:T(8,128)(2,1)S(1)}, u32[]{:S(2)}, u32[]{:S(2)}) async-start(bf16[8,64,2560]{2,1,0:T(8,128)(2,1)} %bitcast.99), calls=%async_computation.5 | async-start | bytes 5242880 | tf_op jit(solution)/shard_map/all_to_all | solution.py:109
  130.8 497.3 %all-gather.9.cloned.1.call-start = ((), (), s32[]{:S(2)}) async-start(), calls=%async_computation.13 | async-start | bytes 10485760 | tf_op jit(solution)/shard_map/all_gather | solution.py:202
  236.2 59.4 %all-to-all-start.6 = ((bf16[8,20,16,512]{3,2,1,0:T(8,128)(2,1)}), bf16[8,20,16,512]{3,2,1,0:T(8,128)(2,1)}, u32[]{:S(2)}, u32[]{:S(2)}) async-start(bf16[8,20,16,512]{3,2,1,0:T(8,128)(2,1)} %bitcast.102), calls=%async_computation.6 | async-start | bytes 5242880 | tf_op jit(solution)/shard_map/all_to_all | solution.py:109
  295.6 4.6 copy-start.22
  295.6 63.3 %all-to-all-start.1 = ((bf16[8,64,2560]{2,1,0:T(8,128)(2,1)}), bf16[8,64,2560]{2,1,0:T(8,128)(2,1)}, u32[]{:S(2)}, u32[]{:S(2)}) async-start(bf16[8,64,2560]{2,1,0:T(8,128)(2,1)} %bitcast.101), calls=%async_computation.1 | async-start | bytes 5242880 | tf_op jit(solution)/shard_map/all_to_all | solution.py:109
  300.3 63.7 %copy-start.13 = (bf16[128,128]{1,0:T(8,128)(2,1)}, bf16[128,128]{1,0:T(8,128)(2,1)S(1)}, u32[]{:S(2)}) copy-start(bf16[128,128]{1,0:T(8,128)(2,1)S(1)} %subtract_convert_fusion.3.refs_5_) | copy-start | bytes 98308
  301.4 5.3 copy-start.6
  304.4 59.6 %copy-start.8 = (bf16[512,512]{1,0:T(8,128)(2,1)}, bf16[512,512]{1,0:T(8,128)(2,1)S(1)}, u32[]{:S(2)}) copy-start(bf16[512,512]{1,0:T(8,128)(2,1)S(1)} %get-tuple-element.30.refs_4_) | copy-start | bytes 1572868
  312.4 1.5 copy-start.2
  313.9 1.5 copy-start.5
  359.0 63.4 %all-to-all-start.7 = ((bf16[8,64,2560]{2,1,0:T(8,128)(2,1)}), bf16[8,64,2560]{2,1,0:T(8,128)(2,1)}, u32[]{:S(2)}, u32[]{:S(2)}) async-start(bf16[8,64,2560]{2,1,0:T(8,128)(2,1)} %bitcast.92), calls=%async_computation.7 | async-start | bytes 5242880 | tf_op jit(solution)/shard_map/all_to_all | solution.py:109
  363.4 281.1 %all-gather.11.cloned.1.call-start = ((), (), s32[]{:S(2)}) async-start(), calls=%async_computation.14 | async-start | bytes 10485760 | tf_op jit(solution)/shard_map/all_gather | solution.py:203
  364.0 1.7 copy-start
  365.7 1.0 copy-start.11
  373.3 1.5 copy-start.4
  422.4 4.6 copy-start.19
  422.4 63.5 %all-to-all-start.2 = ((bf16[8,64,2560]{2,1,0:T(8,128)(2,1)}), bf16[8,64,2560]{2,1,0:T(8,128)(2,1)}, u32[]{:S(2)}, u32[]{:S(2)}) async-start(bf16[8,64,2560]{2,1,0:T(8,128)(2,1)} %bitcast.91), calls=%async_computation.2 | async-start | bytes 5242880 | tf_op jit(solution)/shard_map/all_to_all | solution.py:109
  427.0 0.7 copy-start.18
  485.9 120.4 %all-to-all-start.8 = ((bf16[2,4,8,128,160]{3,2,0,4,1:T(8,128)(2,1)}), bf16[2,4,8,128,160]{3,2,0,4,1:T(8,128)(2,1)}, u32[]{:S(2)}, u32[]{:S(2)}) async-start(bf16[2,4,8,128,160]{3,2,0,4,1:T(8,128)(2,1)} %copy.61), calls=%async_computation.8 | async-start | bytes 5242880 | tf_op jit(solution)/shard_map/all_to_all | solution.py:221
  524.6 14.4 %copy-start.20 = (f32[1,64,160]{2,1,0:T(8,128)S(1)}, f32[1,64,160]{2,1,0:T(8,128)}, u32[]{:S(2)}) copy-start(f32[1,64,160]{2,1,0:T(8,128)} %get-tuple-element.19) | copy-start | bytes 122884
  628.1 8.3 copy-start.16
  628.1 8.3 copy-start.17
  712.8 44.9 %all-to-all-start.3 = ((bf16[2,1,8,128,640]{3,2,0,1,4:T(8,128)(2,1)}), bf16[2,1,8,128,640]{3,2,0,1,4:T(8,128)(2,1)}, u32[]{:S(2)}, u32[]{:S(2)}) async-start(bf16[2,1,8,128,640]{3,2,0,1,4:T(8,128)(2,1)} %multiply_convert_fusion.2), calls=%async_computation.3 | async-start | bytes 5242880 | tf_op jit(solution)/shard_map/all_to_all | solution.py:240
  757.8 64.8 %all-to-all-start.9 = ((bf16[8,64,2560]{2,1,0:T(8,128)(2,1)}), bf16[8,64,2560]{2,1,0:T(8,128)(2,1)}, u32[]{:S(2)}, u32[]{:S(2)}) async-start(bf16[8,64,2560]{2,1,0:T(8,128)(2,1)} %reshape.186), calls=%async_computation.9 | async-start | bytes 5242880 | tf_op jit(solution)/shard_map/all_to_all | solution.py:109
  822.6 4.6 copy-start.14
  822.6 64.2 %all-to-all-start.4 = ((bf16[8,64,2560]{2,1,0:T(8,128)(2,1)}), bf16[8,64,2560]{2,1,0:T(8,128)(2,1)}, u32[]{:S(2)}, u32[]{:S(2)}) async-start(bf16[8,64,2560]{2,1,0:T(8,128)(2,1)} %bitcast.103), calls=%async_computation.4 | async-start | bytes 5242880 | tf_op jit(solution)/shard_map/all_to_all | solution.py:109
  827.1 129.8 %reduce-scatter.2.cloned.1.call-start = ((), (), s32[]{:S(2)}) async-start(), calls=%async_computation.15 | async-start | bytes 294912 | tf_op jit(solution)/shard_map/reduce_scatter | solution.py:266
  827.2 1.7 copy-start.1
  828.9 1.0 copy-start.9
  830.0 1.0 copy-start.12
  831.0 55.7 %copy-start.7 = (bf16[512,512]{1,0:T(8,128)(2,1)S(1)}, bf16[512,512]{1,0:T(8,128)(2,1)}, u32[]{:S(2)}) copy-start(bf16[512,512]{1,0:T(8,128)(2,1)} %copy-done.6) | copy-start | bytes 1572868
  886.7 1.7 copy-start.3
  888.5 1.0 copy-start.10
Sparse Core Ops, SparseCore 0:
  9.5 54.8 all-gather.4
  66.5 103.4 all-gather.6
  228.1 57.4 all-gather.8
  365.5 59.4 all-gather.10
  896.8 60.0 reduce-scatter.1

commit v3 on v2

v3 whole, which is shorter than its diff:
```python
import functools

import jax
import jax.numpy as jnp
from jax import lax
from jax.experimental import pallas as pl
from jax.experimental.pallas import tpu as pltpu
from jax.sharding import PartitionSpec as P

D = 4096
FF = 10240


def hadamard(size, dtype):
    index = jnp.arange(size, dtype=jnp.int32)
    anded = jnp.bitwise_and(index[:, None], index[None, :])
    parity = jnp.zeros((size, size), jnp.int32)
    for bit in range(max(size.bit_length() - 1, 0)):
        parity = jnp.bitwise_xor(parity, jnp.bitwise_and(jnp.right_shift(anded, bit), 1))
    return (1 - 2 * parity).astype(dtype)


def gelu_pair(value):
    argument = 0.7978845608028654 * (value + 0.044715 * value * value * value)
    tangent = jnp.tanh(argument)
    slope = 0.5 * (1.0 + tangent) + 0.5 * value * (1.0 - tangent * tangent) * 0.7978845608028654 * (
        1.0 + 0.134145 * value * value
    )
    return 0.5 * value * (1.0 + tangent), slope


def contract(left, right, left_dim, right_dim):
    return lax.dot_general(
        left, right, (((left_dim,), (right_dim,)), ((), ())), preferred_element_type=jnp.float32
    )


def hadamard_rows(order, size):
    anded = jnp.bitwise_and(order[:, None], jnp.arange(size, dtype=jnp.int32)[None, :])
    parity = jnp.zeros(anded.shape, jnp.int32)
    for bit in range(max(size.bit_length() - 1, 0)):
        parity = jnp.bitwise_xor(parity, jnp.bitwise_and(jnp.right_shift(anded, bit), 1))
    return (1 - 2 * parity).astype(jnp.bfloat16)


def load_vector(ref, at):
    parts, _, inner, width = ref.shape
    item = ref[:, at]
    if inner % 16:
        return item.astype(jnp.float32).reshape(parts * inner, width).astype(item.dtype)
    return item.reshape(parts * inner, width)


def forward_kernel(some, scale_in, scale_out, s_ref, g_ref, sub_ref, rows_ref, tall_ref, wide_ref, e_ref, u_ref):
    width = wide_ref.shape[0]
    sub = sub_ref[...]
    for at in range(some):
        lifted = load_vector(s_ref, at) * sub
        u_ref[at * width : (at + 1) * width, :] = contract(wide_ref[...], lifted, 1, 1).astype(
            jnp.bfloat16
        )
    turned = contract(u_ref[...], rows_ref[...], 1, 1) * scale_in
    mixed = (g_ref[...].astype(jnp.float32) * turned).astype(jnp.bfloat16)
    u_ref[...] = contract(mixed, tall_ref[...], 1, 0).astype(jnp.bfloat16)
    for at in range(some):
        wide = contract(u_ref[at * width : (at + 1) * width, :], wide_ref[...], 0, 0)
        wide = (wide * scale_out).reshape(e_ref.shape[0], *e_ref.shape[2:])
        e_ref[:, at] = wide.astype(jnp.bfloat16)


def adjoint_kernel(some, scale_out, b_ref, s_ref, g_ref, rows_ref, tall_ref, wide_ref, sum_ref, u_ref):
    width = wide_ref.shape[0]

    @pl.when(pl.program_id(0) == 0)
    def _():
        sum_ref[...] = jnp.zeros_like(sum_ref)

    for at in range(some):
        u_ref[at * width : (at + 1) * width, :] = contract(
            wide_ref[...], load_vector(b_ref, at), 1, 1
        ).astype(jnp.bfloat16)
    spread = contract(u_ref[...], tall_ref[...], 1, 0)
    spread = (g_ref[...].astype(jnp.float32) * spread).astype(jnp.bfloat16)
    u_ref[...] = contract(spread, rows_ref[...], 1, 0).astype(jnp.bfloat16)
    total = jnp.zeros(sum_ref.shape, jnp.float32)
    for at in range(some):
        wide = contract(u_ref[at * width : (at + 1) * width, :], wide_ref[...], 0, 0)
        total += load_vector(s_ref, at).astype(jnp.float32) * wide
    sum_ref[...] += total * scale_out


def vectors_at_once(count):
    return max(some for some in range(1, 6) if count % some == 0)


def chain(kernel, operands, whole, result, width, blocks_all, count, summed):
    some = vectors_at_once(count)
    parts = next(item.shape[0] for item in operands if item.ndim == 4)
    flat = pl.BlockSpec((parts, some, blocks_all // parts, width), lambda i: (0, i, 0, 0))
    turned = pl.BlockSpec((some * width, blocks_all), lambda i: (i, 0))
    specs = [flat if item.ndim == 4 else turned for item in operands]
    specs += [pl.BlockSpec(item.shape, lambda i: (0, 0)) for item in whole]
    flops = 2 * count * width * blocks_all * (2 * blocks_all + 2 * width)
    return pl.pallas_call(
        functools.partial(kernel, some),
        grid=(count // some,),
        in_specs=specs,
        out_specs=pl.BlockSpec((blocks_all, width), lambda i: (0, 0)) if summed else flat,
        out_shape=result,
        scratch_shapes=[pltpu.VMEM((some * width, blocks_all), jnp.bfloat16)],
        compiler_params=pltpu.CompilerParams(vmem_limit_bytes=40 * 1024 * 1024),
        cost_estimate=pl.CostEstimate(
            flops=flops, bytes_accessed=6 * count * width * blocks_all, transcendentals=0
        ),
    )(*operands, *whole)


def exchange(item):
    return lax.all_to_all(item, "fsdp", split_axis=0, concat_axis=0, tiled=True)


def on_device(
    tokens,
    cotangent,
    gate_base,
    up_base,
    out_base,
    subspace,
    sign_flips,
    fast_gains,
    fast_scales,
    block_orders,
):
    parts, groups = lax.axis_size("fsdp"), lax.axis_size("dp")
    mine = lax.axis_index("dp")
    _, inner, width, vectors = sign_flips.shape
    blocks_all, some = fast_gains.shape[1], fast_gains.shape[2]
    share = vectors // groups
    hidden_here = gate_base.shape[1]
    direct = hidden_here % vectors == 0
    runs = hidden_here // vectors if direct else 1
    piece = hidden_here // (runs * groups)
    owned = runs * piece

    factors = (D ** (-0.5), FF ** (-0.5))
    slab = (inner, width, vectors)

    def k_slice(item):
        return lax.dynamic_slice_in_dim(item, mine * share, share, axis=item.ndim - 1)

    def of_matrix(item, which):
        start = (which, 0, 0, mine * share)
        return lax.dynamic_slice(item, start, (1,) + item.shape[1:3] + (share,))[0]

    def hidden_columns(item):
        cuts = [
            lax.dynamic_slice_in_dim(item, run * vectors + mine * piece, piece, axis=1)
            for run in range(runs)
        ]
        return jnp.concatenate(cuts, axis=1) if runs > 1 else cuts[0]

    count = -(-share // parts)
    wide_h, tall_h = hadamard(width, jnp.bfloat16), hadamard(blocks_all, jnp.bfloat16)
    rows_h = [hadamard_rows(block_orders[which], blocks_all) for which in range(2)]
    sub_all = exchange(
        jnp.broadcast_to(subspace.astype(jnp.bfloat16), (parts, inner, width))
    ).reshape(blocks_all, width)

    def filled(item, axis):
        if count * parts == share:
            return item
        sides = [(0, 0)] * item.ndim
        sides[axis] = (0, count * parts - share)
        return jnp.pad(item, sides)

    def to_owners(item):
        return exchange(filled(item, 0).reshape(parts, count, inner, width))

    def sign_payload(which):
        return of_matrix(sign_flips, which).astype(jnp.bfloat16).transpose(2, 0, 1)

    def gains_to_owners(which):
        item = filled(of_matrix(fast_gains, which), 2).reshape(blocks_all, some, parts, count)
        item = exchange(item.transpose(2, 3, 1, 0))
        return item.transpose(1, 0, 2, 3).reshape(count * width, blocks_all)

    def weights_home(item):
        return exchange(item).reshape(parts * count, inner, width)[:share]

    def expand(which, signs, gains):
        return chain(
            lambda some, *refs: forward_kernel(
                some,
                (blocks_all * width) ** (-0.5),
                (blocks_all * width) ** (-0.5),
                *refs,
            ),
            (signs, gains),
            (sub_all, rows_h[which], tall_h, wide_h),
            jax.ShapeDtypeStruct((parts, count, inner, width), jnp.bfloat16),
            width,
            blocks_all,
            count,
            False,
        )

    def scaled(item, which):
        own = k_slice(fast_scales[which]).T[:, :, None] * factors[which]
        return (item.astype(jnp.float32) * own).astype(jnp.bfloat16)

    gains_0 = gains_to_owners(0)
    signs_0 = to_owners(sign_payload(0))
    payload, gains_0 = lax.optimization_barrier((sign_payload(1), gains_0))
    gains_1 = gains_to_owners(1)
    home_0 = weights_home(expand(0, signs_0, gains_0))

    x = lax.all_gather(tokens, "fsdp", axis=0, tiled=True)
    dy = lax.all_gather(cotangent, "fsdp", axis=0, tiled=True)
    x, dy, gains_1 = lax.optimization_barrier((x, dy, gains_1))
    x = lax.all_gather(x, "dp", axis=0, tiled=True)
    dy = lax.all_gather(dy, "dp", axis=0, tiled=True)

    up_own = hidden_columns(up_base)
    gate_own = hidden_columns(gate_base) if direct else gate_base
    out_own = lax.dynamic_index_in_dim(
        out_base.reshape(runs, groups, piece, D), mine, 1, keepdims=False
    ).reshape(owned, D)
    payload, home_0, up_own, gate_own, out_own = lax.optimization_barrier(
        (payload, home_0, up_own, gate_own, out_own)
    )
    signs_1 = to_owners(payload)

    delta_gate = scaled(home_0, 0).transpose(1, 2, 0)
    if direct:
        gate_weight = gate_own + delta_gate.reshape(D, owned)
    else:
        delta_gate = lax.all_gather(delta_gate, "dp", axis=2, tiled=True)
        gate_weight = hidden_columns(gate_own + delta_gate.reshape(gate_own.shape))
    gate_weight, signs_1 = lax.optimization_barrier((gate_weight, signs_1))
    signs, gains = (signs_0, signs_1), (gains_0, gains_1)

    strip = inner // (runs * groups)
    home_1 = weights_home(expand(1, signs_1, gains_1))

    gate = jnp.dot(x, gate_weight, preferred_element_type=jnp.float32)
    up = jnp.dot(x, up_own, preferred_element_type=jnp.float32)
    bent, slope = gelu_pair(gate)
    hidden = (bent * up).astype(jnp.bfloat16)
    back_factor = (blocks_all * width) ** (-0.5)
    strips = lax.dynamic_index_in_dim(
        fast_scales[1].reshape(runs, groups, strip, vectors), mine, 1, keepdims=False
    ).reshape(runs * strip, vectors)
    out_grad = contract(hidden, dy, 0, 0).astype(jnp.bfloat16)
    out_grad = out_grad.reshape(runs * strip, width, vectors).transpose(2, 0, 1)
    out_grad = out_grad.astype(jnp.float32) * (strips.T[:, :, None] * (factors[1] * back_factor))
    out_grad = out_grad.astype(jnp.bfloat16)
    home_1, out_grad = lax.optimization_barrier((home_1, out_grad))
    back_out = lax.all_to_all(
        out_grad.reshape(groups, share, runs, strip, width), "dp", split_axis=0, concat_axis=0, tiled=True
    )
    back_out = back_out.transpose(1, 2, 0, 3, 4).reshape(share, inner, width)

    delta_out = scaled(home_1, 1).reshape(share, runs, groups, strip, width)
    delta_out = lax.all_to_all(
        delta_out.transpose(2, 0, 1, 3, 4), "dp", split_axis=0, concat_axis=0, tiled=True
    )
    delta_out = delta_out.reshape(vectors, runs * strip, width).transpose(1, 2, 0)
    out_weight = out_own + delta_out.reshape(owned, D)
    hidden_grad = contract(dy, out_weight, 1, 1)
    gate_grad = (hidden_grad * up * slope).astype(jnp.bfloat16)

    in_grad = contract(x, gate_grad, 0, 0).astype(jnp.bfloat16)
    if direct:
        in_grad = in_grad.reshape(inner, width, share)
    else:
        in_grad = lax.all_gather(in_grad, "dp", axis=1, tiled=True)
        in_grad = k_slice(in_grad.reshape(slab))
    back_gate = scaled(in_grad.transpose(2, 0, 1), 0) * jnp.bfloat16(back_factor)

    def fold(back, which):
        return chain(
            lambda some, *refs: adjoint_kernel(some, (blocks_all * width) ** (-0.5), *refs),
            (to_owners(back), signs[which], gains[which]),
            (rows_h[which], tall_h, wide_h),
            jax.ShapeDtypeStruct((blocks_all, width), jnp.float32),
            width,
            blocks_all,
            count,
            True,
        )

    result = fold(back_out, 1) + fold(back_gate, 0)
    result = jnp.sum(exchange(result.reshape(parts, inner, width)), axis=0)
    return lax.psum(result, "dp")


def solution(mesh):
    in_specs = (
        P(("dp", "fsdp"), None),
        P(("dp", "fsdp"), None),
        P(None, "fsdp"),
        P(None, "fsdp"),
        P("fsdp", None),
        P("fsdp", None),
        P(None, "fsdp", None, None),
        P(None, None, "fsdp", None),
        P(None, "fsdp", None),
        P(),
    )
    out_specs = P("fsdp", None)
    return jax.shard_map(
        on_device, mesh=mesh, in_specs=in_specs, out_specs=out_specs, check_vma=False
    )
```

time: 989 us -> 790 us (0.80)
  local copies, waits for them, and re-layouts: 340 us -> 140 us
  blocking collectives: 105 us -> 58 us
  waiting for transfers between devices: 358 us -> 389 us
  starting transfers between devices: 47.8 us -> 60.1 us
  other arithmetic: 41.4 us -> 53.5 us
    all_gather x1 -> x0, blocking collectives: 93.5 us -> none  [on_device(): lax.all_gather(subspace.astype(jnp.bfloat16), 'fsdp', axis=0, tiled=True)]
    all_to_all x8 -> x9, waiting for transfers between devices: 296 us -> 366 us  [exchange(): return lax.all_to_all(item, 'fsdp', split_axis=0, concat_axis=0, tiled=True)]
    reduce_scatter x1 -> x0, waiting for transfers between devices: 60.2 us -> none  [on_device(): result = lax.psum_scatter(result, 'fsdp', scatter_dimension=0, tiled=True)]
    unnamed x53 -> x32, local copies, waits for them, and re-layouts: 77.5 us -> 28.8 us
    all_to_all x0 -> x2, blocking collectives: none -> 47.1 us  [the longest x1 34.6 us: on_device(): lax.all_to_all(delta_out.transpose(2, 0, 1, 3, 4), 'dp', split_axis=0, co...]
    slice x2 -> x0, local copies, waits for them, and re-layouts: 46.3 us -> none  [the longest x1 29.2 us: signs_to_owners(): item = filled(k_slice(sign_flips[which]).astype(jnp.bfloat16))]
    reshape x8 -> x2, local copies, waits for them, and re-layouts: 59.2 us -> 12.9 us  [the longest x1 7.3 us: on_device(): gate_weight = gate_own + delta_gate.reshape(D, owned)]
    convert_element_type x7 -> x4, local copies, waits for them, and re-layouts: 67.3 us -> 27.3 us  [the longest x2 15.3 us: scaled(): return (item.astype(jnp.float32) * own).astype(jnp.bfloat16)]
  transfers between devices with their start and end apart: 15 -> 14, of which waited for: 8 -> 9; matrix products, arithmetic and copies ran while one was open for 35% -> 28% of each run, Pallas kernels for 2% -> 3%
where the time goes in v3:
time: 790 us; the launch traced here: 780 us
  waiting for transfers between devices  389 us (49%)
  local copies, waits for them, and re-layouts  140 us (18%)
  starting transfers between devices  60.1 us (8%)
  blocking collectives  58 us (7%)
  other arithmetic  53.5 us (7%)
  matrix products  39.3 us (5%)
  Pallas kernels  26 us (3%)
  between operations  13.8 us (2%)
    all_to_all x9, waiting for transfers between devices, exchange(): return lax.all_to_all(item, 'fsdp', split_axis=0, concat_axis=0, tiled=True)  366 us
    all_to_all x9, starting transfers between devices, exchange(): return lax.all_to_all(item, 'fsdp', split_axis=0, concat_axis=0, tiled=True)  55.2 us
    all_to_all x1, blocking collectives, on_device(): lax.all_to_all(delta_out.transpose(2, 0, 1, 3, 4), 'dp', split_axis=0, co...  34.6 us
    unnamed x32, local copies, waits for them, and re-layouts  28.8 us
    dot_general x3, matrix products, contract(): lax.dot_general(left, right, (((left_dim,), (right_dim,)), ((), ())), pre...  26.8 us
    pallas_call x4, Pallas kernels, chain(): pl.pallas_call(functools.partial(kernel, some), grid=(count // some,), in...  26 us
    all_gather x1, waiting for transfers between devices, on_device(): dy = lax.all_gather(cotangent, 'fsdp', axis=0, tiled=True)  21.6 us
  transfers between devices with their start and end apart: 14, of which 9 were waited for; matrix products, arithmetic and copies ran while one was open for 28% of the time, Pallas kernels for 3%

profile of v3, /device:TPU:0, one launch (start us, length us, event | category | flops | bytes accessed | tf_op | source)
XLA Modules:
  0.0 780.3 jit_solution(16183156827426583921)
XLA Ops:
  7.3 12.4 %constant_dynamic-slice_fusion = (bf16[1,512,16,160]{3,2,1,0:T(8,128)(2,1)}, bf16[1,512,16,160]{3,2,1,0:T(8,128)(2,1)}) fusion(bf16[2,512,16,640]{3,2,1,0:T(8,128)(2,1)} %param.17, s32[]{:T(128)S(6)} %select_n.11), kind=kLoop, calls=%fused_computation.41 | loop fusion | bytes 10485764 | tf_op jit(solution)/shard_map/dynamic_slice | solution.py:153
  19.7 8.1 %copy.79 = bf16[1,512,16,160]{1,2,3,0:T(8,128)(2,1)} copy(bf16[1,512,16,160]{3,2,1,0:T(8,128)(2,1)} %get-tuple-element.35) | data formatting | bytes 5242880
  27.8 7.3 all-to-all-start.5
  35.9 84.0 %all-to-all-done.5 = bf16[8,20,16,512]{3,2,1,0:T(8,128)(2,1)S(1)} async-done(((bf16[8,20,16,512]{3,2,1,0:T(8,128)(2,1)}), bf16[8,20,16,512]{3,2,1,0:T(8,128)(2,1)S(1)}, u32[]{:S(2)}, u32[]{:S(2)}) %all-to-all-start.5) | async-done | bytes 2621472 | tf_op jit(solution)/shard_map/all_to_all | solution.py:119
  121.4 2.3 copy.68
  123.8 21.6 %all-gather.7.cloned.1.call-done = bf16[256,4096]{1,0:T(8,128)(2,1)} async-done(((bf16[32,4096]{1,0:T(8,128)(2,1)}), bf16[256,4096]{1,0:T(8,128)(2,1)}) %all-gather.7.cloned.1.call-update) | async-done | bytes 2097168 | tf_op jit(solution)/shard_map/all_gather | solution.py:218
  146.1 3.4 all-to-all-start.2
  149.5 8.5 %copy.77 = bf16[1,512,16,160]{1,2,3,0:T(8,128)(2,1)} copy(bf16[1,512,16,160]{3,2,1,0:T(8,128)(2,1)} %get-tuple-element.36) | data formatting | bytes 5242880
  157.9 5.9 all-to-all-start
  163.8 13.6 %fusion.5 = (bf16[160,64,128]{0,2,1:T(8,128)(2,1)}, bf16[160,64,128]{0,2,1:T(8,128)(2,1)}) fusion(s32[2,64,128,640]{3,2,1,0:T(8,128)} %param.16, s32[]{:T(128)S(6)} %select_n.11), kind=kLoop, calls=%fused_computation.13 | loop fusion | flops 2621440 | bytes 15728644 | tf_op jit(solution)/shard_map/transpose | solution.py:180
  177.5 6.3 copy.63
  183.8 38.7 %all-to-all-done = bf16[8,20,16,512]{3,2,1,0:T(8,128)(2,1)} async-done(((bf16[8,20,16,512]{3,2,1,0:T(8,128)(2,1)}), bf16[8,20,16,512]{3,2,1,0:T(8,128)(2,1)}, u32[]{:S(2)}, u32[]{:S(2)}) %all-to-all-start) | async-done | bytes 2621472 | tf_op jit(solution)/shard_map/all_to_all | solution.py:119
  222.5 4.8 all-to-all-start.1
  227.4 3.0 subtract_convert_fusion.1
  230.4 3.6 copy.62
  233.9 52.3 %all-to-all-done.1.refs_0_.refs_1_ = bf16[8,20,64,128]{3,2,1,0:T(8,128)(2,1)} async-done(((bf16[8,20,64,128]{3,2,1,0:T(8,128)(2,1)}), bf16[8,20,64,128]{3,2,1,0:T(8,128)(2,1)}, u32[]{:S(2)}, u32[]{:S(2)}) %all-to-all-start.1) | async-done | bytes 2621472 | tf_op jit(solution)/shard_map/all_to_all | solution.py:119
  286.3 1.7 copy-done
  289.1 6.5 shard_map.100
  295.6 1.5 copy-done.2
  297.1 4.4 all-to-all-start.3
  302.1 3.5 constant_dynamic-slice_fusion.1
  305.6 10.4 %constant_dynamic-slice_fusion.3 = (bf16[4096,160]{1,0:T(8,128)(2,1)S(1)}, bf16[4096,160]{1,0:T(8,128)(2,1)S(1)}, bf16[4096,160]{1,0:T(8,128)(2,1)S(1)}, bf16[4096,160]{1,0:T(8,128)(2,1)}) fusion(bf16[4096,1280]{1,0:T(8,128)(2,1)} %param.12, s32[]{:T(128)S(6)} %select_n.13, s32[]{:T(128)S(6)} %select_n.14, bf16[4096,1280]{1,0:T(8,128)(2,1)} %param.13), kind=kLoop, calls=%fused_computation.44 | loop fusion | bytes 10485768 | tf_op jit(solution)/shard_map/dynamic_slice | solution.py:157
  316.1 4.9 pad_maximum_fusion
  320.9 2.9 pad_maximum_fusion.1
  323.8 36.7 %all-to-all-done.3 = bf16[8,20,64,128]{3,2,1,0:T(8,128)(2,1)} async-done(((bf16[8,20,64,128]{3,2,1,0:T(8,128)(2,1)}), bf16[8,20,64,128]{3,2,1,0:T(8,128)(2,1)}, u32[]{:S(2)}, u32[]{:S(2)}) %all-to-all-start.3) | async-done | bytes 2621472 | tf_op jit(solution)/shard_map/all_to_all | solution.py:119
  360.5 6.3 copy.66
  366.8 16.2 %all-to-all-start.4 = ((bf16[8,20,64,128]{3,2,1,0:T(8,128)(2,1)}), bf16[8,20,64,128]{3,2,1,0:T(8,128)(2,1)}, u32[]{:S(2)}, u32[]{:S(2)}) async-start(bf16[8,20,64,128]{3,2,1,0:T(8,128)(2,1)} %bitcast.80), calls=%async_computation.4 | async-start | bytes 5242880 | tf_op jit(solution)/shard_map/all_to_all | solution.py:119
  384.8 1.9 subtract_convert_fusion.refs_3_
  386.6 6.8 copy.65
  393.4 5.6 fusion.6
  399.0 7.3 reshape.81
  406.3 5.4 add.55
  411.7 30.1 %all-to-all-done.4.refs_0_.refs_1_ = bf16[8,20,64,128]{3,2,1,0:T(8,128)(2,1)} async-done(((bf16[8,20,64,128]{3,2,1,0:T(8,128)(2,1)}), bf16[8,20,64,128]{3,2,1,0:T(8,128)(2,1)}, u32[]{:S(2)}, u32[]{:S(2)}) %all-to-all-start.4) | async-done | bytes 2621472 | tf_op jit(solution)/shard_map/all_to_all | solution.py:119
  442.9 6.5 shard_map.101
  450.9 4.4 all-to-all-start.6
  456.9 1.6 copy.72
  458.5 8.5 %fusion.29 = f32[1024,320]{0,1:T(8,128)} fusion(bf16[1024,4096]{1,0:T(8,128)(2,1)} %all-gather.9.cloned.1.call-done, bf16[4096,320]{1,0:T(8,128)(2,1)} %add.55), kind=kOutput, calls=%fused_computation.54 | convolution fusion | flops 2684354560 | bytes 12320768 | tf_op jit(solution)/shard_map/dot_general | solution.py:245
  466.9 4.1 fusion.30
  471.0 9.6 %fusion.2 = f32[320,4096]{1,0:T(8,128)} fusion(bf16[1024,4096]{1,0:T(8,128)(2,1)} %all-gather.11.cloned.1.call-done, f32[1024,320]{0,1:T(8,128)} %fusion.30, f32[1024,320]{0,1:T(8,128)} %fusion.29), kind=kOutput, calls=%fused_computation.8 | convolution fusion | flops 2690252800 | bytes 16252928 | tf_op jit(solution)/shard_map/dot_general | solution.py:33
  480.6 5.8 reshape.91
  486.4 6.2 copy.69
  492.6 4.4 fusion.3
  497.0 17.2 %all-to-all-done.6 = bf16[8,20,64,128]{3,2,1,0:T(8,128)(2,1)} async-done(((bf16[8,20,64,128]{3,2,1,0:T(8,128)(2,1)}), bf16[8,20,64,128]{3,2,1,0:T(8,128)(2,1)}, u32[]{:S(2)}, u32[]{:S(2)}) %all-to-all-start.6) | async-done | bytes 2621472 | tf_op jit(solution)/shard_map/all_to_all | solution.py:119
  514.2 3.5 multiply_convert_fusion.1
  518.2 34.6 %all_to_all.60 = bf16[4,160,2,8,128]{4,3,2,1,0:T(8,128)(2,1)} all-to-all(bf16[4,160,2,8,128]{4,3,2,1,0:T(8,128)(2,1)S(1)} %copy.73), channel_id=1, replica_groups=mesh['dp'=4,'fsdp'=8] {'dp'}, dimensions={0} | all-to-all | bytes 5242880 | tf_op jit(solution)/shard_map/all_to_all | solution.py:264
  552.8 4.7 all-to-all-start.7
  557.6 4.8 copy.74
  562.4 5.6 reshape.88
  568.0 9.2 %fusion.16 = bf16[1024,320]{0,1:T(8,128)(2,1)S(1)} fusion(f32[1024,320]{0,1:T(8,128)} %fusion.29, f32[1024,320]{0,1:T(8,128)} %fusion.30, bf16[1024,4096]{1,0:T(8,128)(2,1)} %all-gather.11.cloned.1.call-done, bf16[320,4096]{1,0:T(8,128)(2,1)} %bitcast.89, bf16[320,4096]{1,0:T(8,128)(2,1)} %reshape.88), kind=kOutput, calls=%fused_computation.28 | convolution fusion | flops 2692218880 | bytes 16908288 | tf_op jit(solution)/shard_map/dot_general | solution.py:33
  577.1 8.0 %fusion.1 = f32[4096,320]{0,1:T(8,128)} fusion(bf16[1024,320]{0,1:T(8,128)(2,1)S(1)} %fusion.16, bf16[1024,4096]{1,0:T(8,128)(2,1)} %all-gather.9.cloned.1.call-done), kind=kOutput, calls=%fused_computation.6 | convolution fusion | flops 2686976000 | bytes 14286848 | tf_op jit(solution)/shard_map/dot_general | solution.py:33
  585.1 6.3 copy.75
  591.5 9.0 %reshape.92 = f32[64,128,160]{2,1,0:T(8,128)} reshape(f32[4096,320]{1,0:T(8,128)} %copy.75) | data formatting | bytes 10485760 | tf_op jit(solution)/shard_map/convert_element_type | solution.py:209
  600.5 6.8 fusion.7
  607.3 6.3 copy.76
  613.6 4.4 all-to-all-start.10
  618.0 4.0 copy.71
  622.0 56.4 %all-to-all-done.10.refs_0_ = bf16[8,20,64,128]{3,2,1,0:T(8,128)(2,1)} async-done(((bf16[8,20,64,128]{3,2,1,0:T(8,128)(2,1)}), bf16[8,20,64,128]{3,2,1,0:T(8,128)(2,1)}, u32[]{:S(2)}, u32[]{:S(2)}) %all-to-all-start.10) | async-done | bytes 2621472 | tf_op jit(solution)/shard_map/all_to_all | solution.py:119
  678.4 4.4 all-to-all-start.8
  682.8 1.7 copy-done.1
  685.6 6.5 shard_map.103
  692.1 50.3 %all-to-all-done.8.refs_0_ = bf16[8,20,64,128]{3,2,1,0:T(8,128)(2,1)} async-done(((bf16[8,20,64,128]{3,2,1,0:T(8,128)(2,1)}), bf16[8,20,64,128]{3,2,1,0:T(8,128)(2,1)}, u32[]{:S(2)}, u32[]{:S(2)}) %all-to-all-start.8) | async-done | bytes 2621472 | tf_op jit(solution)/shard_map/all_to_all | solution.py:119
  743.5 6.5 shard_map.102
  750.0 12.5 %all_to_all.61 = f32[8,64,128]{2,1,0:T(8,128)S(1)} all-to-all(f32[8,64,128]{2,1,0:T(8,128)S(1)} %bitcast.90), channel_id=1, replica_groups=mesh['dp'=4,'fsdp'=8] {'fsdp'}, dimensions={0} | all-to-all | bytes 524288 | tf_op jit(solution)/shard_map/all_to_all | solution.py:119
  762.5 10.9 %psum.7 = f32[64,128]{1,0:T(8,128)} all-reduce(f32[64,128]{1,0:T(8,128)S(1)} %reduce_sum.9), channel_id=1, replica_groups=mesh['dp'=4,'fsdp'=8] {'dp'}, use_global_device_ids=true, to_apply=%region_1.2 | all-reduce | flops 8192 | bytes 65536 | tf_op jit(solution)/shard_map/psum | solution.py:294
  (51 shorter events, 13.9 us)
Async XLA Ops:
  6.5 117.2 %all-gather.5.cloned.1.call-start = ((), (), s32[]{:S(2)}) async-start(), calls=%async_computation.12 | async-start | bytes 2359296 | tf_op jit(solution)/shard_map/all_gather | solution.py:217
  27.8 92.1 %all-to-all-start.5 = ((bf16[8,20,16,512]{3,2,1,0:T(8,128)(2,1)}), bf16[8,20,16,512]{3,2,1,0:T(8,128)(2,1)S(1)}, u32[]{:S(2)}, u32[]{:S(2)}) async-start(bf16[8,20,16,512]{3,2,1,0:T(8,128)(2,1)} %bitcast.83), calls=%async_computation.5 | async-start | bytes 5242880 | tf_op jit(solution)/shard_map/all_to_all | solution.py:119
  35.1 110.2 %all-gather.7.cloned.1.call-start = ((), (), s32[]{:S(2)}) async-start(), calls=%async_computation.13 | async-start | bytes 2359296 | tf_op jit(solution)/shard_map/all_gather | solution.py:218
  35.9 422.6 %all-gather.9.cloned.1.call-start = ((), (), s32[]{:S(2)}) async-start(), calls=%async_computation.14 | async-start | bytes 10485760 | tf_op jit(solution)/shard_map/all_gather | solution.py:220
  119.9 1.5 copy-start.8
  121.4 23.9 %copy-start.12 = (f32[64,128]{1,0:T(8,128)S(1)}, f32[64,128]{1,0:T(8,128)}, u32[]{:S(2)}) copy-start(f32[64,128]{1,0:T(8,128)} %param.15) | copy-start | bytes 98308
  146.1 11.8 %all-to-all-start.2 = ((bf16[8,64,128]{2,1,0:T(8,128)(2,1)}), bf16[8,64,128]{2,1,0:T(8,128)(2,1)S(1)}, u32[]{:S(2)}, u32[]{:S(2)}) async-start(bf16[8,64,128]{2,1,0:T(8,128)(2,1)} %broadcast_in_dim.2), calls=%async_computation.2 | async-start | bytes 262144 | tf_op jit(solution)/shard_map/all_to_all | solution.py:119
  157.9 64.6 %all-to-all-start = ((bf16[8,20,16,512]{3,2,1,0:T(8,128)(2,1)}), bf16[8,20,16,512]{3,2,1,0:T(8,128)(2,1)}, u32[]{:S(2)}, u32[]{:S(2)}) async-start(bf16[8,20,16,512]{3,2,1,0:T(8,128)(2,1)} %bitcast.84), calls=%async_computation | async-start | bytes 5242880 | tf_op jit(solution)/shard_map/all_to_all | solution.py:119
  222.5 4.9 copy-start.13
  222.5 63.8 %all-to-all-start.1 = ((bf16[8,20,64,128]{3,2,1,0:T(8,128)(2,1)}), bf16[8,20,64,128]{3,2,1,0:T(8,128)(2,1)}, u32[]{:S(2)}, u32[]{:S(2)}) async-start(bf16[8,20,64,128]{3,2,1,0:T(8,128)(2,1)} %bitcast.81), calls=%async_computation.1 | async-start | bytes 5242880 | tf_op jit(solution)/shard_map/all_to_all | solution.py:119
  286.3 1.7 copy-start
  288.0 1.0 copy-start.4
  295.6 1.5 copy-start.2
  297.1 63.4 %all-to-all-start.3 = ((bf16[8,20,64,128]{3,2,1,0:T(8,128)(2,1)}), bf16[8,20,64,128]{3,2,1,0:T(8,128)(2,1)}, u32[]{:S(2)}, u32[]{:S(2)}) async-start(bf16[8,20,64,128]{3,2,1,0:T(8,128)(2,1)} %copy-done.2), calls=%async_computation.3 | async-start | bytes 5242880 | tf_op jit(solution)/shard_map/all_to_all | solution.py:119
  301.5 169.5 %all-gather.11.cloned.1.call-start = ((), (), s32[]{:S(2)}) async-start(), calls=%async_computation.15 | async-start | bytes 10485760 | tf_op jit(solution)/shard_map/all_gather | solution.py:221
  366.8 75.1 %all-to-all-start.4 = ((bf16[8,20,64,128]{3,2,1,0:T(8,128)(2,1)}), bf16[8,20,64,128]{3,2,1,0:T(8,128)(2,1)}, u32[]{:S(2)}, u32[]{:S(2)}) async-start(bf16[8,20,64,128]{3,2,1,0:T(8,128)(2,1)} %bitcast.80), calls=%async_computation.4 | async-start | bytes 5242880 | tf_op jit(solution)/shard_map/all_to_all | solution.py:119
  384.8 8.6 %copy-start.10 = (f32[160,64]{0,1:T(8,128)}, f32[160,64]{0,1:T(8,128)S(1)}, u32[]{:S(2)}) copy-start(f32[160,64]{0,1:T(8,128)S(1)} %get-tuple-element.46) | copy-start | bytes 122884
  441.9 1.0 copy-start.6
  449.4 1.5 copy-start.3
  450.9 63.3 %all-to-all-start.6 = ((bf16[8,20,64,128]{3,2,1,0:T(8,128)(2,1)}), bf16[8,20,64,128]{3,2,1,0:T(8,128)(2,1)}, u32[]{:S(2)}, u32[]{:S(2)}) async-start(bf16[8,20,64,128]{3,2,1,0:T(8,128)(2,1)} %copy-done.3), calls=%async_computation.6 | async-start | bytes 5242880 | tf_op jit(solution)/shard_map/all_to_all | solution.py:119
  458.5 8.5 %copy-start.9 = (bf16[4096,320]{1,0:T(8,128)(2,1)S(1)}, bf16[4096,320]{1,0:T(8,128)(2,1)}, u32[]{:S(2)}) copy-start(bf16[4096,320]{1,0:T(8,128)(2,1)} %pad_maximum_fusion) | copy-start | bytes 7864324
  458.5 8.5 %copy-start.14 = (bf16[1024,4096]{1,0:T(8,128)(2,1)S(1)}, bf16[1024,4096]{1,0:T(8,128)(2,1)}, u32[]{:S(2)}) copy-start(bf16[1024,4096]{1,0:T(8,128)(2,1)} %all-gather.9.cloned.1.call-done) | copy-start | bytes 25165828
  552.8 60.8 %all-to-all-start.7 = ((bf16[4,160,2,8,128]{4,3,2,1,0:T(8,128)(2,1)}), bf16[4,160,2,8,128]{4,3,2,1,0:T(8,128)(2,1)}, u32[]{:S(2)}, u32[]{:S(2)}) async-start(bf16[4,160,2,8,128]{4,3,2,1,0:T(8,128)(2,1)} %bitcast.79), calls=%async_computation.7 | async-start | bytes 5242880 | tf_op jit(solution)/shard_map/all_to_all | solution.py:258
  591.5 9.0 %copy-start.11 = (f32[160,64]{0,1:T(8,128)S(1)}, f32[160,64]{0,1:T(8,128)}, u32[]{:S(2)}) copy-start(f32[160,64]{0,1:T(8,128)} %copy-done.10) | copy-start | bytes 122884
  613.6 64.8 %all-to-all-start.10 = ((bf16[8,20,64,128]{3,2,1,0:T(8,128)(2,1)}), bf16[8,20,64,128]{3,2,1,0:T(8,128)(2,1)}, u32[]{:S(2)}, u32[]{:S(2)}) async-start(bf16[8,20,64,128]{3,2,1,0:T(8,128)(2,1)} %bitcast.86), calls=%async_computation.10 | async-start | bytes 5242880 | tf_op jit(solution)/shard_map/all_to_all | solution.py:119
  678.4 64.0 %all-to-all-start.8 = ((bf16[8,20,64,128]{3,2,1,0:T(8,128)(2,1)}), bf16[8,20,64,128]{3,2,1,0:T(8,128)(2,1)}, u32[]{:S(2)}, u32[]{:S(2)}) async-start(bf16[8,20,64,128]{3,2,1,0:T(8,128)(2,1)} %bitcast.85), calls=%async_computation.8 | async-start | bytes 5242880 | tf_op jit(solution)/shard_map/all_to_all | solution.py:119
  682.8 1.7 copy-start.1
  684.5 1.0 copy-start.5
  742.4 1.0 copy-start.7
Sparse Core Ops, SparseCore 0:
  9.5 67.5 all-gather.4
  79.2 66.1 all-gather.6
  146.9 56.7 all-gather.8
  303.6 59.5 all-gather.10
